TPU v7x, 512 devices: a whole 4x8x8 slice. The times are simulated.
512 devices in a mesh: uly: 16 (over y_hi, x, core), blk: 32 (over y_lo, z).
Axes of the slice: x: 4, y: 8 (y_hi: 2, y_lo: 4; y = y_hi * 4 + y_lo), z: 8, core: 2. Of those that a mesh axis runs over, the one named last changes fastest.
Arguments:
- tokens: bfloat16 [32, 2048, 3072], P('blk', 'uly'), may hold values from -18 to 18
- query_weight: bfloat16 [3072, 32, 128], P('blk', 'uly'), may hold values from -0.109375 to 0.109375
- key_values: bfloat16 [32, 2048, 32, 256], P('blk', 'uly'), may hold values from -18 to 18
Outputs:
- attended: bfloat16 [32, 2048, 32, 128], P('blk', 'uly')
All inputs are finite; a program needn't handle non-finite values.
Results may differ from a plain program's by a relative error of at most 0.012.
Values may be sent and summed in bfloat16 or wider, within the bound.
No kernel may reach another device: no remote copies, remote signals or barrier semaphores. Data moves between devices by JAX's collectives and lax.ppermute only.
A program may use at most 64 MiB of HBM per device.

v0:
```python
import jax
import jax.numpy as jnp
from jax import lax
from jax.sharding import PartitionSpec as P


def attend_heads(queries, head_kv, head_width):
    row_count = queries.shape[0]
    head_count = queries.shape[1]
    key_rows = head_kv[:, :, :head_width]
    value_rows = head_kv[:, :, head_width:]
    score_scale = head_width ** (-0.5)
    block_rows = min(512, row_count)
    query_blocks = queries.reshape(row_count // block_rows, block_rows, head_count, head_width)

    def attend(query_block):
        scores = (
            jnp.einsum("qhd,khd->hqk", query_block, key_rows, preferred_element_type=jnp.float32)
            * score_scale
        )
        row_max = jnp.max(scores, axis=2, keepdims=True)
        soft = jnp.exp(scores - row_max)
        row_sum = jnp.sum(soft, axis=2)
        weighted = jnp.einsum(
            "hqk,khd->qhd",
            soft.astype(jnp.bfloat16),
            value_rows,
            preferred_element_type=jnp.float32,
        )
        return (weighted / jnp.transpose(row_sum)[:, :, None]).astype(jnp.bfloat16)

    return lax.map(attend, query_blocks).reshape(row_count, head_count, head_width)


def body(tokens, query_weight, key_values):
    local_tokens = tokens[0]
    shard_rows = query_weight.shape[0]
    head_count = query_weight.shape[1]
    head_width = query_weight.shape[2]
    flat_weight = query_weight.reshape(shard_rows, head_count * head_width)
    gathered = lax.all_gather(local_tokens, "uly", axis=0, tiled=True)
    projected = jnp.dot(
        gathered,
        lax.all_gather(flat_weight, "blk", axis=0, tiled=True),
        preferred_element_type=jnp.float32,
    )
    row_count = projected.shape[0]
    queries = projected.astype(jnp.bfloat16).reshape(row_count, head_count, head_width)
    head_kv = lax.all_to_all(key_values[0], "uly", split_axis=1, concat_axis=0, tiled=True)
    normalized = attend_heads(queries, head_kv, head_width)
    returned = lax.all_to_all(normalized, "uly", split_axis=0, concat_axis=1, tiled=True)
    return returned[None]


def solution(mesh):
    return jax.shard_map(
        body,
        mesh=mesh,
        in_specs=(P("blk", "uly", None), P("blk", "uly", None), P("blk", "uly", None, None)),
        out_specs=P("blk", "uly", None, None),
        check_vma=False,
    )
```

profile of v0, /device:TPU:16, one launch (start us, length us, event | category | flops | bytes accessed | tf_op | source)
XLA Modules:
  0.0 416.6 jit_solution(1167986095403846415)
XLA Ops:
  6.5 0.0 all-gather.4.cloned.1.call-start
  6.5 1.4 copy.33
  8.0 0.0 all-gather.4.cloned.1.call-update
  8.0 0.0 all-gather.6.cloned.1.call-start
  8.0 0.7 all-gather.6.cloned.1.call-update
  8.7 4.1 copy.32
  12.8 7.9 %all-to-all-start = ((bf16[128,32,256]{2,0,1:T(8,128)(2,1)}), bf16[128,32,256]{2,0,1:T(8,128)(2,1)S(1)}, u32[]{:S(2)}, u32[]{:S(2)}) async-start(bf16[128,32,256]{2,0,1:T(8,128)(2,1)} %bitcast.59), calls=%async_computation | async-start | bytes 4194304 | tf_op jit(solution)/shard_map/all_to_all | solution.py:49
  20.7 58.3 %all-to-all-done = bf16[128,32,256]{2,0,1:T(8,128)(2,1)S(1)} async-done(((bf16[128,32,256]{2,0,1:T(8,128)(2,1)}), bf16[128,32,256]{2,0,1:T(8,128)(2,1)S(1)}, u32[]{:S(2)}, u32[]{:S(2)}) %all-to-all-start) | async-done | bytes 2097184 | tf_op jit(solution)/shard_map/all_to_all | solution.py:49
  79.0 0.1 copy.15
  79.2 1.4 fusion.28
  80.6 87.5 %all-gather.4.cloned.1.call-done = bf16[3072,256]{1,0:T(8,128)(2,1)} async-done(((bf16[96,256]{1,0:T(8,128)(2,1)}), bf16[3072,256]{1,0:T(8,128)(2,1)}) %all-gather.4.cloned.1.call-update) | async-done | bytes 1572880 | tf_op jit(solution)/shard_map/all_gather | solution.py:44
  168.0 163.8 %all-gather.6.cloned.1.call-done = bf16[1,2048,3072]{2,1,0:T(8,128)(2,1)} async-done(((bf16[1,128,3072]{2,1,0:T(8,128)(2,1)}), bf16[1,2048,3072]{2,1,0:T(8,128)(2,1)}) %all-gather.6.cloned.1.call-update) | async-done | bytes 12582928 | tf_op jit(solution)/shard_map/all_gather | solution.py:41
  331.9 9.4 %fusion.25 = bf16[2048,256]{1,0:T(8,128)(2,1)} fusion(bf16[3072,256]{1,0:T(8,128)(2,1)} %all-gather.4.cloned.1.call-done, bf16[1,2048,3072]{2,1,0:T(8,128)(2,1)} %all-gather.6.cloned.1.call-done), kind=kOutput, calls=%fused_computation.18 | convolution fusion | flops 3221749760 | bytes 15204352 | tf_op jit(solution)/shard_map/dot_general | solution.py:42
  341.3 1.3 reshape_reshape.3
  342.7 20.2 %while.10 = (s32[]{:T(128)}, bf16[4,512,2,128]{3,1,0,2:T(8,128)(2,1)S(1)}, bf16[4,512,2,128]{3,2,1,0:T(2,128)(2,1)S(1)}, bf16[2048,2,128]{2,0,1:T(8,128)(2,1)S(1)}, bf16[2048,2,128]{2,0,1:T(8,128)(2,1)}, /*index=5*/s32[]{:T(128)}) while((s32[]{:T(128)}, bf16[4,512,2,128]{3,1,0,2:T(8,128)(2,1)S(1)}, bf16[4,512,2,128]{3,2,1,0:T(2,128)(2,1)S(1)}, ...), condition=%wide.region_3.4_spmd, body=%wide.region_0.3_spmd.sunk | while | flops 1090779136 | bytes 32526448 | solution.py:32
  342.7 0.2 constant_dynamic-slice_fusion.2
  342.9 0.0 copy-start
  342.9 1.3 multiply_reduce_fusion.2
  344.2 1.6 fusion.40
  345.9 0.0 copy-done
  345.9 1.8 fusion.41
  347.7 0.2 constant_dynamic-slice_fusion.2
  347.9 0.0 copy-start
  347.9 1.3 multiply_reduce_fusion.2
  349.3 1.6 fusion.40
  350.9 0.0 copy-done
  350.9 1.8 fusion.41
  352.7 0.2 constant_dynamic-slice_fusion.2
  352.9 0.0 copy-start
  353.0 1.3 multiply_reduce_fusion.2
  354.3 1.6 fusion.40
  355.9 0.0 copy-done
  355.9 1.8 fusion.41
  357.8 0.2 constant_dynamic-slice_fusion.2
  358.0 0.0 copy-start
  358.0 1.3 multiply_reduce_fusion.2
  359.3 1.6 fusion.40
  361.0 0.0 copy-done
  361.0 1.8 fusion.41
  362.8 8.7 %copy.18 = bf16[2048,2,128]{2,1,0:T(2,128)(2,1)S(1)} copy(bf16[2048,2,128]{2,0,1:T(8,128)(2,1)S(1)} %bitcast.63) | data formatting | bytes 2097152 | tf_op jit(solution)/shard_map/reshape | solution.py:32
  371.5 36.4 %all_to_all.33 = bf16[2048,2,128]{2,1,0:T(2,128)(2,1)S(1)} all-to-all(bf16[2048,2,128]{2,1,0:T(2,128)(2,1)S(1)} %copy.18), channel_id=1, replica_groups=mesh['uly'=16,'blk'=32] {'uly'}, dimensions={0} | all-to-all | bytes 2097152 | tf_op jit(solution)/shard_map/all_to_all | solution.py:51
  407.9 0.1 copy.19
  408.0 0.1 copy.20
  408.1 1.7 copy.21
  (1 shorter events, 0.0 us)
Async XLA Ops:
  6.5 161.5 %all-gather.4.cloned.1.call-start = ((), (), s32[]{:S(2)}) async-start(), calls=%async_computation.2 | async-start | bytes 1622016 | tf_op jit(solution)/shard_map/all_gather | solution.py:44
  8.0 323.9 %all-gather.6.cloned.1.call-start = ((), (), s32[]{:S(2)}) async-start(), calls=%async_computation.3 | async-start | bytes 13369344 | tf_op jit(solution)/shard_map/all_gather | solution.py:41
  12.8 66.2 %all-to-all-start = ((bf16[128,32,256]{2,0,1:T(8,128)(2,1)}), bf16[128,32,256]{2,0,1:T(8,128)(2,1)S(1)}, u32[]{:S(2)}, u32[]{:S(2)}) async-start(bf16[128,32,256]{2,0,1:T(8,128)(2,1)} %bitcast.59), calls=%async_computation | async-start | bytes 4194304 | tf_op jit(solution)/shard_map/all_to_all | solution.py:49
  342.9 3.0 copy-start
  347.9 3.0 copy-start
  352.9 3.0 copy-start
  358.0 3.0 copy-start
Sparse Core Ops, SparseCore 0:
  9.4 158.5 all-gather.3
  171.4 160.4 all-gather.5
where the time goes:
time: 417 us
  waiting for transfers between devices  310 us (74%)
  blocking collectives  36.4 us (9%)
  matrix products  22.1 us (5%)
  local copies, waits for them, and re-layouts  19.7 us (5%)
  between operations  13.5 us (3%)
  starting transfers between devices  7.91 us (2%)
  other arithmetic  6.56 us (2%)
    all_gather x1, waiting for transfers between devices, body(): gathered = lax.all_gather(local_tokens, 'uly', axis=0, tiled=True)  164 us
    all_gather x1, waiting for transfers between devices, body(): lax.all_gather(flat_weight, 'blk', axis=0, tiled=True)  87.5 us
    all_to_all x1, waiting for transfers between devices, body(): lax.all_to_all(key_values[0], 'uly', split_axis=1, concat_axis=0, tiled=T...  58.3 us
    all_to_all x1, blocking collectives, body(): lax.all_to_all(normalized, 'uly', split_axis=0, concat_axis=1, tiled=True)  36.4 us
    dot_general x1, matrix products, body(): jnp.dot(gathered, lax.all_gather(flat_weight, 'blk', axis=0, tiled=True),...  9.41 us
    reshape x1, local copies, waits for them, and re-layouts, attend_heads(): lax.map(attend, query_blocks).reshape(row_count, head_count, head_width)  8.68 us
  transfers between devices with their start and end apart: 3, of which 3 were waited for; matrix products, arithmetic and copies ran while one was open for 1% of the time, Pallas kernels for 0%

commit v1 on v0

v1 whole, which is shorter than its diff:
```python
import jax
import jax.numpy as jnp
from jax import lax
from jax.sharding import PartitionSpec as P

HALVES = 2
GROUP = 8
RUNS = 4
RING = 8


def half_groups():
    return [[half * GROUP + member for member in range(GROUP)] for half in range(HALVES)]


def along_z(step):
    return [(run * RING + z, run * RING + (z + step) % RING) for run in range(RUNS) for z in range(RING)]


def other_half(array):
    pairs = [(member, (member + GROUP) % (HALVES * GROUP)) for member in range(HALVES * GROUP)]
    return lax.ppermute(array, "uly", pairs)


def within_half(array):
    return lax.all_to_all(array, "uly", 0, 0, tiled=True, axis_index_groups=half_groups())


def gather_weight(flat_weight):
    rows, width = flat_weight.shape
    pairs = [[member, member + GROUP] for member in range(GROUP)]
    both = lax.all_gather(flat_weight, "uly", axis=1, tiled=True, axis_index_groups=pairs)
    runs = [[run * RING + z for run in range(RUNS)] for z in range(RING)]
    block = lax.all_gather(both, "blk", axis=0, axis_index_groups=runs)
    rings = [[run * RING + z for z in range(RING)] for run in range(RUNS)]
    whole = lax.all_gather(block, "blk", axis=1, axis_index_groups=rings)
    return whole.reshape(RUNS * RING * rows, HALVES * width)


def attend_head(query, keys, values):
    scores = jnp.dot(query, keys.T, preferred_element_type=jnp.float32) * (query.shape[1] ** -0.5)
    row_max = jnp.max(scores, axis=1, keepdims=True)
    soft = jnp.exp(scores - row_max)
    row_sum = jnp.sum(soft, axis=1, keepdims=True)
    weighted = jnp.dot(soft.astype(jnp.bfloat16), values, preferred_element_type=jnp.float32)
    return (weighted / row_sum).astype(jnp.bfloat16)


def body(tokens, query_weight, key_values):
    rows, pair, width = query_weight.shape
    local_tokens, local_kv = tokens[0], key_values[0]
    token_count, head_count = local_kv.shape[0], local_kv.shape[1]
    slots = HALVES * pair

    spread = jnp.transpose(local_kv.reshape(token_count, HALVES, GROUP, pair, 2 * width), (2, 1, 3, 0, 4))
    spread = spread.reshape(GROUP, slots, token_count, 2 * width)
    near = within_half(spread)
    near = [near[:, slot].reshape(GROUP * token_count, 2 * width) for slot in range(slots)]
    far = [other_half(part) for part in near]

    gathered = lax.all_gather(local_tokens, "uly", axis=0, tiled=True, axis_index_groups=half_groups())
    weight = gather_weight(query_weight.reshape(rows, pair * width))
    queries = jnp.dot(gathered, weight, preferred_element_type=jnp.float32).astype(jnp.bfloat16)

    outs = []
    for slot in range(slots):
        kv = jnp.concatenate([near[slot], far[slot]], axis=0)
        query = queries[:, slot * width : (slot + 1) * width]
        outs.append(attend_head(query, kv[:, :width], kv[:, width:]).reshape(GROUP, token_count, width))
    first = within_half(jnp.stack(outs[:-1], axis=1))
    last = within_half(outs[-1])
    heads = jnp.concatenate([first, last[:, None]], axis=1).reshape(GROUP, HALVES, pair, token_count, width)
    return jnp.transpose(heads, (3, 1, 0, 2, 4)).reshape(1, token_count, head_count, width)


def solution(mesh):
    return jax.shard_map(
        body,
        mesh=mesh,
        in_specs=(P("blk", "uly", None), P("blk", "uly", None), P("blk", "uly", None, None)),
        out_specs=P("blk", "uly", None, None),
        check_vma=False,
    )
```

time: 417 us -> 228 us (0.55)
  the two profiles are of different devices: /device:TPU:16 before, /device:TPU:1 now
where the time goes in v1:
time: 228 us; the launch traced here: 227 us
  blocking collectives  76.8 us (34%)
  waiting for transfers between devices  72.7 us (32%)
  matrix products  26.7 us (12%)
  starting transfers between devices  23.1 us (10%)
  between operations  13.5 us (6%)
  other arithmetic  7.91 us (3%)
  local copies, waits for them, and re-layouts  6.04 us (3%)
    all_to_all x2, blocking collectives, within_half(): lax.all_to_all(array, 'uly', 0, 0, tiled=True, axis_index_groups=half_gro...  54.9 us
    all_gather x1, waiting for transfers between devices, body(): lax.all_gather(local_tokens, 'uly', axis=0, tiled=True, axis_index_groups...  43.6 us
    ppermute x4, waiting for transfers between devices, other_half(): return lax.ppermute(array, 'uly', pairs)  28.4 us
    ppermute x4, starting transfers between devices, other_half(): return lax.ppermute(array, 'uly', pairs)  18.4 us
    all_gather x1, blocking collectives, gather_weight(): block = lax.all_gather(both, 'blk', axis=0, axis_index_groups=runs)  13.4 us
    dot_general x4, matrix products, attend_head(): jnp.dot(soft.astype(jnp.bfloat16), values, preferred_element_type=jnp.flo...  10.5 us
    dot_general x4, matrix products, attend_head(): jnp.dot(query, keys.T, preferred_element_type=jnp.float32)  9.11 us
    all_gather x1, blocking collectives, gather_weight(): lax.all_gather(flat_weight, 'uly', axis=1, tiled=True, axis_index_groups=...  8.61 us
  transfers between devices with their start and end apart: 7, of which 2 were waited for; matrix products, arithmetic and copies ran while one was open for 17% of the time, Pallas kernels for 0%

profile of v1, /device:TPU:1, one launch (start us, length us, event | category | flops | bytes accessed | tf_op | source)
XLA Modules:
  0.0 226.9 jit_solution(16947852334752452221)
XLA Ops:
  6.5 0.0 all-gather.8.cloned.1.call-start
  6.5 0.8 copy.17
  7.3 8.6 %all_gather.19 = bf16[96,512]{1,0:T(8,128)(2,1)S(1)} all-gather(bf16[96,256]{1,0:T(8,128)(2,1)S(1)} %bitcast.55), channel_id=1, replica_groups={{0,256},{32,288},{64,320},{96,352},{128,384},{160,416},{192,448},{224,4..., dimensions={1}, use_global_device_ids=true | all-gather | bytes 147456 | tf_op jit(solution)/shard_map/all_gather | solution.py:32
  16.0 13.4 %all-gather.1 = bf16[384,512]{1,0:T(8,128)(2,1)} all-gather(bf16[96,512]{1,0:T(8,128)(2,1)S(1)} %all_gather.19), channel_id=3, replica_groups={{0,8,16,24},{1,9,17,25},{2,10,18,26},{3,11,19,27},{4,12,20,28},{5,13,21..., dimensions={0}, use_global_device_ids=true | all-gather | bytes 491520 | tf_op jit(solution)/shard_map/all_gather | solution.py:34
  29.3 0.0 all-gather.8.cloned.1.call-update
  29.3 0.0 all-gather.6.cloned.1.call-start
  29.4 0.7 all-gather.6.cloned.1.call-update
  30.1 2.8 %copy.9 = bf16[1,128,32,256]{3,1,2,0:T(8,128)(2,1)S(1)} copy(bf16[1,128,32,256]{3,2,1,0:T(8,128)(2,1)} %param.5) | data formatting | bytes 4194304 | tf_op args[2]
  32.9 0.2 copy.10
  33.1 38.0 %all_to_all.15 = bf16[8,4,128,256]{3,2,1,0:T(8,128)(2,1)S(1)} all-to-all(bf16[8,4,128,256]{3,2,1,0:T(8,128)(2,1)S(1)} %bitcast.35), channel_id=1, replica_groups={{0,32,64,96,128,160,192,224},{256,288,320,352,384,416,448,480},{1,33,65..., dimensions={0} | all-to-all | bytes 4194304 | tf_op jit(solution)/shard_map/all_to_all | solution.py:26
  71.1 0.2 fusion.77
  71.3 4.6 %collective-permute-start = (bf16[1024,256]{1,0:T(8,128)(2,1)S(1)}, bf16[1024,256]{1,0:T(8,128)(2,1)}, u32[]{:S(2)}, u32[]{:S(2)}) collective-permute-start(bf16[1024,256]{1,0:T(8,128)(2,1)S(1)} %bitcast.44), channel_id=1, source_target_pairs={{0,256},{32,288},{64,320},{96,352},{128,384},{160,416},{192,448},{... | collective-permute-start | bytes 1572872 | tf_op jit(solution)/shard_map/ppermute | solution.py:22
  76.0 4.6 %collective-permute-start.1 = (bf16[1024,256]{1,0:T(8,128)(2,1)S(1)}, bf16[1024,256]{1,0:T(8,128)(2,1)}, u32[]{:S(2)}, u32[]{:S(2)}) collective-permute-start(bf16[1024,256]{1,0:T(8,128)(2,1)S(1)} %bitcast.41), channel_id=1, source_target_pairs={{0,256},{32,288},{64,320},{96,352},{128,384},{160,416},{192,448},{... | collective-permute-start | bytes 1572872 | tf_op jit(solution)/shard_map/ppermute | solution.py:22
  80.5 4.6 %collective-permute-start.2 = (bf16[1024,256]{1,0:T(8,128)(2,1)S(1)}, bf16[1024,256]{1,0:T(8,128)(2,1)}, u32[]{:S(2)}, u32[]{:S(2)}) collective-permute-start(bf16[1024,256]{1,0:T(8,128)(2,1)S(1)} %bitcast.38), channel_id=1, source_target_pairs={{0,256},{32,288},{64,320},{96,352},{128,384},{160,416},{192,448},{... | collective-permute-start | bytes 1572872 | tf_op jit(solution)/shard_map/ppermute | solution.py:22
  85.2 4.6 %collective-permute-start.3 = (bf16[1024,256]{1,0:T(8,128)(2,1)S(1)}, bf16[1024,256]{1,0:T(8,128)(2,1)}, u32[]{:S(2)}, u32[]{:S(2)}) collective-permute-start(bf16[1024,256]{1,0:T(8,128)(2,1)S(1)} %bitcast.47), channel_id=1, source_target_pairs={{0,256},{32,288},{64,320},{96,352},{128,384},{160,416},{192,448},{... | collective-permute-start | bytes 1572872 | tf_op jit(solution)/shard_map/ppermute | solution.py:22
  89.7 0.0 all-gather.8.cloned.1.call-done
  89.8 43.6 %all-gather.6.cloned.1.call-done = bf16[1,1024,3072]{2,1,0:T(8,128)(2,1)} async-done(((bf16[1,128,3072]{2,1,0:T(8,128)(2,1)}), bf16[1,1024,3072]{2,1,0:T(8,128)(2,1)}) %all-gather.6.cloned.1.call-update) | async-done | bytes 6291472 | tf_op jit(solution)/shard_map/all_gather | solution.py:61
  133.4 7.1 %fusion.18 = bf16[1024,512]{1,0:T(8,128)(2,1)S(1)} fusion(bf16[3072,512]{1,0:T(8,128)(2,1)} %bitcast.57, bf16[1,1024,3072]{2,1,0:T(8,128)(2,1)} %all-gather.6.cloned.1.call-done), kind=kOutput, calls=%fused_computation.22 | convolution fusion | flops 3221749760 | bytes 10485760 | tf_op jit(solution)/shard_map/dot_general | solution.py:63
  140.5 28.4 %collective-permute-done.3 = bf16[1024,256]{1,0:T(8,128)(2,1)} collective-permute-done((bf16[1024,256]{1,0:T(8,128)(2,1)S(1)}, bf16[1024,256]{1,0:T(8,128)(2,1)}, u32[]{:S(2)}, u32[]{:S(2)}) %collective-permute-start.3) | collective-permute-done | bytes 524320 | tf_op jit(solution)/shard_map/ppermute | solution.py:22
  168.9 2.3 %multiply_reduce_fusion = (f32[1024]{0:T(1024)S(1)}, f32[1024,2048]{1,0:T(8,128)S(1)}) fusion(bf16[1024,256]{1,0:T(8,128)(2,1)S(1)} %bitcast.48, bf16[1024,256]{1,0:T(8,128)(2,1)} %collective-permute-done.3, bf16[1024,512]{1,0:T(8,128)(2,1)S(1)} %fusion.18), kind=kOutput, calls=%fused_computation.4 | convolution fusion | flops 542112768 | bytes 9703424 | tf_op jit(solution)/shard_map/dot_general | solution.py:41
  171.2 1.9 fusion.6
  173.1 3.2 %fusion.42 = bf16[1024,128]{1,0:T(8,128)(2,1)} fusion(f32[1024,2048]{1,0:T(8,128)S(1)} %get-tuple-element.10, f32[1024]{0:T(1024)S(1)} %get-tuple-element.9, bf16[1024,256]{1,0:T(8,128)(2,1)} %collective-permute-done.3, bf16[1024,256]{1,0:T(8,128)(2,1)S(1)} %bitcast.49, f32[1024]{0:T(1024)S(1)} %fusion.6), kind=kOutput, calls=%fused_computation.39 | convolution fusion | flops 544473088 | bytes 9707520 | tf_op jit(solution)/shard_map/dot_general | solution.py:45
  176.3 4.7 %all-to-all-start.2 = ((bf16[8,128,128]{2,1,0:T(8,128)(2,1)}), bf16[8,128,128]{2,1,0:T(8,128)(2,1)S(1)}, u32[]{:S(2)}, u32[]{:S(2)}) async-start(bf16[8,128,128]{2,1,0:T(8,128)(2,1)} %bitcast.16), calls=%async_computation.2 | async-start | bytes 524288 | tf_op jit(solution)/shard_map/all_to_all | solution.py:26
  180.9 0.0 collective-permute-done
  180.9 2.3 %multiply_reduce_fusion.3 = (f32[1024]{0:T(1024)S(1)}, f32[1024,2048]{1,0:T(8,128)S(1)}) fusion(bf16[1024,256]{1,0:T(8,128)(2,1)S(1)} %bitcast.45, bf16[1024,256]{1,0:T(8,128)(2,1)} %collective-permute-done, bf16[1024,512]{1,0:T(8,128)(2,1)S(1)} %fusion.18), kind=kOutput, calls=%fused_computation.7 | convolution fusion | flops 542112768 | bytes 9703424 | tf_op jit(solution)/shard_map/dot_general | solution.py:41
  183.2 1.9 fusion
  185.1 0.0 collective-permute-done.1
  185.1 2.3 %multiply_reduce_fusion.2 = (f32[1024]{0:T(1024)S(1)}, f32[1024,2048]{1,0:T(8,128)S(1)}) fusion(bf16[1024,256]{1,0:T(8,128)(2,1)S(1)} %bitcast.42, bf16[1024,256]{1,0:T(8,128)(2,1)} %collective-permute-done.1, bf16[1024,512]{1,0:T(8,128)(2,1)S(1)} %fusion.18), kind=kOutput, calls=%fused_computation.6 | convolution fusion | flops 542112768 | bytes 9703424 | tf_op jit(solution)/shard_map/dot_general | solution.py:41
  187.4 1.9 fusion.2
  189.4 0.0 collective-permute-done.2
  189.4 2.3 %multiply_reduce_fusion.1 = (f32[1024]{0:T(1024)S(1)}, f32[1024,2048]{1,0:T(8,128)S(1)}) fusion(bf16[1024,256]{1,0:T(8,128)(2,1)S(1)} %bitcast.39, bf16[1024,256]{1,0:T(8,128)(2,1)} %collective-permute-done.2, bf16[1024,512]{1,0:T(8,128)(2,1)S(1)} %fusion.18), kind=kOutput, calls=%fused_computation.5 | convolution fusion | flops 542112768 | bytes 9703424 | tf_op jit(solution)/shard_map/dot_general | solution.py:41
  191.6 1.9 fusion.4
  193.6 2.5 %fusion.24 = bf16[1024,128]{1,0:T(8,128)(2,1)S(1)} fusion(f32[1024,2048]{1,0:T(8,128)S(1)} %get-tuple-element.16, f32[1024]{0:T(1024)S(1)} %get-tuple-element.15, bf16[1024,256]{1,0:T(8,128)(2,1)} %collective-permute-done, bf16[1024,256]{1,0:T(8,128)(2,1)S(1)} %bitcast.46, f32[1024]{0:T(1024)S(1)} %fusion), kind=kOutput, calls=%fused_computation.33 | convolution fusion | flops 544473088 | bytes 9707520 | tf_op jit(solution)/shard_map/dot_general | solution.py:45
  196.0 2.5 %fusion.30 = bf16[1024,128]{1,0:T(8,128)(2,1)S(1)} fusion(f32[1024,2048]{1,0:T(8,128)S(1)} %get-tuple-element.14, f32[1024]{0:T(1024)S(1)} %get-tuple-element.13, bf16[1024,256]{1,0:T(8,128)(2,1)} %collective-permute-done.1, bf16[1024,256]{1,0:T(8,128)(2,1)S(1)} %bitcast.43, f32[1024]{0:T(1024)S(1)} %fusion.2), kind=kOutput, calls=%fused_computation.35 | convolution fusion | flops 544473088 | bytes 9707520 | tf_op jit(solution)/shard_map/dot_general | solution.py:45
  198.5 2.5 %fusion.36 = bf16[1024,128]{1,0:T(8,128)(2,1)S(1)} fusion(f32[1024,2048]{1,0:T(8,128)S(1)} %get-tuple-element.12, f32[1024]{0:T(1024)S(1)} %get-tuple-element.11, bf16[1024,256]{1,0:T(8,128)(2,1)} %collective-permute-done.2, bf16[1024,256]{1,0:T(8,128)(2,1)S(1)} %bitcast.40, f32[1024]{0:T(1024)S(1)} %fusion.4), kind=kOutput, calls=%fused_computation.37 | convolution fusion | flops 544473088 | bytes 9707520 | tf_op jit(solution)/shard_map/dot_general | solution.py:45
  200.9 0.1 pad_maximum_fusion.1
  201.0 0.0 all-to-all-done.2
  201.1 16.8 %all_to_all.16 = bf16[8,3,128,128]{3,2,1,0:T(8,128)(2,1)S(1)} all-to-all(bf16[8,3,128,128]{3,2,1,0:T(8,128)(2,1)S(1)} %pad_maximum_fusion.1), channel_id=1, replica_groups={{0,32,64,96,128,160,192,224},{256,288,320,352,384,416,448,480},{1,33,65..., dimensions={0} | all-to-all | bytes 1572864 | tf_op jit(solution)/shard_map/all_to_all | solution.py:26
  217.9 0.1 pad_maximum_fusion
  218.0 2.0 copy.14
Async XLA Ops:
  6.5 83.2 %all-gather.8.cloned.1.call-start = ((), (), s32[]{:S(2)}) async-start(), calls=%async_computation.4 | async-start | bytes 3538944 | tf_op jit(solution)/shard_map/all_gather | solution.py:36
  29.3 104.1 %all-gather.6.cloned.1.call-start = ((), (), s32[]{:S(2)}) async-start(), calls=%async_computation.3 | async-start | bytes 7077888 | tf_op jit(solution)/shard_map/all_gather | solution.py:61
  71.3 109.6 %collective-permute-start = (bf16[1024,256]{1,0:T(8,128)(2,1)S(1)}, bf16[1024,256]{1,0:T(8,128)(2,1)}, u32[]{:S(2)}, u32[]{:S(2)}) collective-permute-start(bf16[1024,256]{1,0:T(8,128)(2,1)S(1)} %bitcast.44), channel_id=1, source_target_pairs={{0,256},{32,288},{64,320},{96,352},{128,384},{160,416},{192,448},{... | collective-permute-start | bytes 1572872 | tf_op jit(solution)/shard_map/ppermute | solution.py:22
  76.0 109.2 %collective-permute-start.1 = (bf16[1024,256]{1,0:T(8,128)(2,1)S(1)}, bf16[1024,256]{1,0:T(8,128)(2,1)}, u32[]{:S(2)}, u32[]{:S(2)}) collective-permute-start(bf16[1024,256]{1,0:T(8,128)(2,1)S(1)} %bitcast.41), channel_id=1, source_target_pairs={{0,256},{32,288},{64,320},{96,352},{128,384},{160,416},{192,448},{... | collective-permute-start | bytes 1572872 | tf_op jit(solution)/shard_map/ppermute | solution.py:22
  80.5 108.8 %collective-permute-start.2 = (bf16[1024,256]{1,0:T(8,128)(2,1)S(1)}, bf16[1024,256]{1,0:T(8,128)(2,1)}, u32[]{:S(2)}, u32[]{:S(2)}) collective-permute-start(bf16[1024,256]{1,0:T(8,128)(2,1)S(1)} %bitcast.38), channel_id=1, source_target_pairs={{0,256},{32,288},{64,320},{96,352},{128,384},{160,416},{192,448},{... | collective-permute-start | bytes 1572872 | tf_op jit(solution)/shard_map/ppermute | solution.py:22
  85.2 83.7 %collective-permute-start.3 = (bf16[1024,256]{1,0:T(8,128)(2,1)S(1)}, bf16[1024,256]{1,0:T(8,128)(2,1)}, u32[]{:S(2)}, u32[]{:S(2)}) collective-permute-start(bf16[1024,256]{1,0:T(8,128)(2,1)S(1)} %bitcast.47), channel_id=1, source_target_pairs={{0,256},{32,288},{64,320},{96,352},{128,384},{160,416},{192,448},{... | collective-permute-start | bytes 1572872 | tf_op jit(solution)/shard_map/ppermute | solution.py:22
  176.3 24.8 %all-to-all-start.2 = ((bf16[8,128,128]{2,1,0:T(8,128)(2,1)}), bf16[8,128,128]{2,1,0:T(8,128)(2,1)S(1)}, u32[]{:S(2)}, u32[]{:S(2)}) async-start(bf16[8,128,128]{2,1,0:T(8,128)(2,1)} %bitcast.16), calls=%async_computation.2 | async-start | bytes 524288 | tf_op jit(solution)/shard_map/all_to_all | solution.py:26
Sparse Core Ops, SparseCore 0:
  29.5 57.0 all-gather.7
  88.7 44.6 all-gather.5

commit v2 on v1

v2 whole, which is shorter than its diff:
```python
import functools

import jax
import jax.numpy as jnp
from jax import lax
from jax.experimental import pallas as pl
from jax.experimental.pallas import tpu as pltpu
from jax.sharding import PartitionSpec as P

HALVES = 2
ALONG_X = 4
CORES = 2
GROUP = ALONG_X * CORES
RUNS = 4
RING = 8
LOG2_E = 1.4426950408889634


def send(array, dy, dx, dc):
    pairs = []
    for half in range(HALVES):
        for x in range(ALONG_X):
            for core in range(CORES):
                target = ((half + dy) % HALVES, (x + dx) % ALONG_X, (core + dc) % CORES)
                pairs.append(((half * ALONG_X + x) * CORES + core, (target[0] * ALONG_X + target[1]) * CORES + target[2]))
    return lax.ppermute(array, "uly", pairs)


def within_half(array):
    groups = [[half * GROUP + member for member in range(GROUP)] for half in range(HALVES)]
    return lax.all_to_all(array, "uly", 0, 0, tiled=True, axis_index_groups=groups)


def spread_weight(copies):
    lines = [
        [(half * GROUP + member) * RUNS * RING + run * RING + z for half in range(HALVES) for run in range(RUNS)]
        for member in range(GROUP)
        for z in range(RING)
    ]
    return lax.all_to_all(copies, ("uly", "blk"), 0, 0, tiled=True, axis_index_groups=lines)


def gather_ring(block):
    rings = [[run * RING + z for z in range(RING)] for run in range(RUNS)]
    return lax.all_gather(block, "blk", axis=0, axis_index_groups=rings)


def project_kernel(tokens_ref, weight_ref, query_ref, whole_ref):
    ring, runs, rows, _ = weight_ref.shape

    @pl.when(pl.program_id(0) == 0)
    def _():
        for run in range(runs):
            for z in range(ring):
                start = (run * ring + z) * rows
                whole_ref[start : start + rows, :] = weight_ref[z, run]

    product = jnp.dot(tokens_ref[...], whole_ref[...], preferred_element_type=jnp.float32)
    slots, _, width = query_ref.shape
    for slot in range(slots):
        query_ref[slot] = product[:, slot * width : (slot + 1) * width].astype(query_ref.dtype)


def project(tokens, weight, slots):
    count, depth = tokens.shape
    columns = weight.shape[-1]
    width = columns // slots
    block = 128
    return pl.pallas_call(
        project_kernel,
        out_shape=jax.ShapeDtypeStruct((slots, count, width), tokens.dtype),
        grid=(count // block,),
        in_specs=[
            pl.BlockSpec((block, depth), lambda i: (i, 0)),
            pl.BlockSpec(weight.shape, lambda i: (0, 0, 0, 0)),
        ],
        out_specs=pl.BlockSpec((slots, block, width), lambda i: (0, i, 0)),
        scratch_shapes=[pltpu.VMEM((depth, columns), weight.dtype)],
        compiler_params=pltpu.CompilerParams(vmem_limit_bytes=32 * 2**20),
    )(tokens, weight)


def attend_kernel(query_ref, *refs):
    out_ref = refs[-1]
    members, rows, width = out_ref.shape
    factor = width**-0.5 * LOG2_E
    parts = [ref[...].reshape(-1, 2 * width) for ref in refs[:-1]]
    keys = [part[:, :width] for part in parts]
    values = [jnp.concatenate([part[:, width:], jnp.ones_like(part[:, width:])], axis=1) for part in parts]
    for member in range(members):
        query = query_ref[0, member]
        scores = [
            lax.dot_general(query, key, (((1,), (1,)), ((), ())), preferred_element_type=jnp.float32) for key in keys
        ]
        row_max = functools.reduce(jnp.maximum, [jnp.max(score, axis=1, keepdims=True) for score in scores])
        summed = 0.0
        for score, value in zip(scores, values):
            soft = jnp.exp2((score - row_max) * factor)
            summed = summed + jnp.dot(soft.astype(value.dtype), value, preferred_element_type=jnp.float32)
        out_ref[member] = (summed[:, :width] / summed[:, width : width + 1]).astype(out_ref.dtype)


def attend(queries, slot, *parts):
    _, members, rows, width = queries.shape
    specs = [pl.BlockSpec((1, members, rows, width), lambda i: (slot, 0, 0, 0))]
    for part, place in parts:
        shape = [1 if axis == place else size for axis, size in enumerate(part.shape)]
        index = [slot % part.shape[place] if axis == place else 0 for axis in range(part.ndim)]
        specs.append(pl.BlockSpec(tuple(shape), functools.partial(lambda index, i: index, tuple(index))))
    return pl.pallas_call(
        attend_kernel,
        out_shape=jax.ShapeDtypeStruct((members, rows, width), queries.dtype),
        grid=(1,),
        in_specs=specs,
        out_specs=pl.BlockSpec((members, rows, width), lambda i: (0, 0, 0)),
        compiler_params=pltpu.CompilerParams(vmem_limit_bytes=32 * 2**20),
    )(queries, *[part for part, _ in parts])


def to_core(parts):
    core = lax.axis_index("uly") % CORES
    mine = lax.dynamic_index_in_dim(parts, core, 0, keepdims=False)
    theirs = lax.dynamic_index_in_dim(parts, 1 - core, 0, keepdims=False)
    return mine, send(theirs, 0, 0, 1)


def to_column(parts):
    x = lax.axis_index("uly") % GROUP // CORES
    out = []
    for dx in range(ALONG_X):
        part = lax.dynamic_index_in_dim(parts, (x + dx) % ALONG_X, 0, keepdims=False)
        out.append(send(part, 0, dx, 0) if dx else part)
    return out


def body(tokens, query_weight, key_values):
    rows, pair, width = query_weight.shape
    local_tokens, local_kv = tokens[0], key_values[0]
    token_count, head_count = local_kv.shape[0], local_kv.shape[1]
    slots = HALVES * pair
    together = lax.optimization_barrier

    groups = [[half * GROUP + member for member in range(GROUP)] for half in range(HALVES)]
    gathered = lax.all_gather(local_tokens, "uly", axis=0, tiled=True, axis_index_groups=groups)
    copies = jnp.broadcast_to(query_weight.reshape(1, rows, pair * width), (HALVES * RUNS, rows, pair * width))
    copies, local_kv = together((copies, local_kv))
    block = spread_weight(copies)

    spread = jnp.transpose(local_kv.reshape(token_count, HALVES, ALONG_X, CORES, pair, 2 * width), (3, 2, 1, 4, 0, 5))
    spread = spread.reshape(CORES, ALONG_X, slots, token_count, 2 * width)
    both = jnp.stack(to_core(spread), axis=2)
    block, both = together((block, both))

    lead = both[:, 0]
    lead_far = send(lead, 1, 0, 0)
    rest = to_column(both[:, 1:])
    near = [jnp.stack([part[slot] for part in rest]) for slot in range(slots - 1)]
    far = [send(keys, 1, 0, 0) for keys in near]
    lead_far, gathered = together((lead_far, gathered))
    early = to_column(jnp.stack([lead, lead_far], axis=1))

    block = jnp.transpose(block.reshape(HALVES, RUNS, rows, pair * width), (1, 2, 0, 3))
    weight = gather_ring(block.reshape(RUNS, rows, slots * width))
    queries = project(gathered, weight, slots).reshape(slots, GROUP, token_count, width)
    outs = [attend(queries, 0, *[(part, None) for part in early])]
    outs += [attend(queries, slot + 1, (near[slot], None), (far[slot], None)) for slot in range(slots - 1)]
    heads = within_half(jnp.stack(outs, axis=1)).reshape(GROUP, HALVES, pair, token_count, width)
    return jnp.transpose(heads, (3, 1, 0, 2, 4)).reshape(1, token_count, head_count, width)


def solution(mesh):
    return jax.shard_map(
        body,
        mesh=mesh,
        in_specs=(P("blk", "uly", None), P("blk", "uly", None), P("blk", "uly", None, None)),
        out_specs=P("blk", "uly", None, None),
        check_vma=False,
    )
```

time: 228 us -> 189 us (0.83)
  blocking collectives: 76.8 us -> 25.4 us
  matrix products: 26.7 us -> 0 us
  starting transfers between devices: 23.1 us -> 46.4 us
  Pallas kernels: 0 us -> 18.5 us
  local copies, waits for them, and re-layouts: 6.04 us -> 23.4 us
  waiting for transfers between devices: 72.7 us -> 56.5 us
  other arithmetic: 7.91 us -> 4.02 us
    all_gather x1, waiting for transfers between devices: 43.6 us -> 0.02 us  [body(): lax.all_gather(local_tokens, 'uly', axis=0, tiled=True, axis_index_groups...]
    all_to_all x2 -> x1, blocking collectives: 54.9 us -> 25.4 us  [within_half(): lax.all_to_all(array, 'uly', 0, 0, tiled=True, axis_index_groups=groups)]
    dot_general x9 -> x0, matrix products: 26.7 us -> none  [the longest x4 10.5 us: attend_head(): jnp.dot(soft.astype(jnp.bfloat16), values, preferred_element_type=jnp.flo...]
    ppermute x4 -> x11, starting transfers between devices: 18.4 us -> 42.9 us  [send(): return lax.ppermute(array, 'uly', pairs)]
    all_gather x2 -> x0, blocking collectives: 22 us -> none  [the longest x1 13.4 us: gather_weight(): block = lax.all_gather(both, 'blk', axis=0, axis_index_groups=runs)]
    all_gather x1, waiting for transfers between devices: 0.02 us -> 19.5 us  [gather_ring(): return lax.all_gather(block, 'blk', axis=0, axis_index_groups=rings)]
    pallas_call x0 -> x5, Pallas kernels: none -> 18.5 us  [the longest x4 13.3 us: attend(): pl.pallas_call(attend_kernel, out_shape=jax.ShapeDtypeStruct((members, ro...]
    all_to_all x1, waiting for transfers between devices: 0.01 us -> 12.6 us  [spread_weight(): lax.all_to_all(copies, ('uly', 'blk'), 0, 0, tiled=True, axis_index_group...]
  transfers between devices with their start and end apart: 7 -> 14, of which waited for: 2 -> 6; matrix products, arithmetic and copies ran while one was open for 17% -> 10% of each run, Pallas kernels for 0% -> 8%
where the time goes in v2:
time: 189 us; the launch traced here: 188 us
  waiting for transfers between devices  56.5 us (30%)
  starting transfers between devices  46.4 us (25%)
  blocking collectives  25.4 us (13%)
  local copies, waits for them, and re-layouts  23.4 us (12%)
  Pallas kernels  18.5 us (10%)
  between operations  13.8 us (7%)
  other arithmetic  4.02 us (2%)
    ppermute x11, starting transfers between devices, send(): return lax.ppermute(array, 'uly', pairs)  42.9 us
    all_to_all x1, blocking collectives, within_half(): lax.all_to_all(array, 'uly', 0, 0, tiled=True, axis_index_groups=groups)  25.4 us
    ppermute x11, waiting for transfers between devices, send(): return lax.ppermute(array, 'uly', pairs)  23.7 us
    all_gather x1, waiting for transfers between devices, gather_ring(): return lax.all_gather(block, 'blk', axis=0, axis_index_groups=rings)  19.5 us
    pallas_call x4, Pallas kernels, attend(): pl.pallas_call(attend_kernel, out_shape=jax.ShapeDtypeStruct((members, ro...  13.3 us
    all_to_all x1, waiting for transfers between devices, spread_weight(): lax.all_to_all(copies, ('uly', 'blk'), 0, 0, tiled=True, axis_index_group...  12.6 us
    unnamed x9, local copies, waits for them, and re-layouts  7.59 us
    pallas_call x1, Pallas kernels, project(): pl.pallas_call(project_kernel, out_shape=jax.ShapeDtypeStruct((slots, cou...  5.27 us
  transfers between devices with their start and end apart: 14, of which 6 were waited for; matrix products, arithmetic and copies ran while one was open for 10% of the time, Pallas kernels for 8%

profile of v2, /device:TPU:1, one launch (start us, length us, event | category | flops | bytes accessed | tf_op | source)
XLA Modules:
  0.0 188.0 jit_solution(1889312729009955686)
XLA Ops:
  6.5 0.7 all-gather.6.cloned.1.call-update
  7.3 0.8 copy.18
  8.1 0.8 broadcast_in_dim.8
  8.9 4.2 %reshape.24 = bf16[128,2,4,2,2,256]{5,4,3,2,1,0:T(2,128)(2,1)} reshape(bf16[128,32,256]{2,1,0:T(8,128)(2,1)} %bitcast.60) | data formatting | bytes 4194304 | tf_op jit(solution)/shard_map/reshape | solution.py:149
  13.1 2.8 %copy.12 = bf16[2,4,2,2,128,256]{5,4,3,2,1,0:T(8,128)(2,1)S(1)} copy(bf16[2,4,2,2,128,256]{5,3,0,1,2,4:T(2,128)(2,1)} %bitcast.58) | data formatting | bytes 4194304 | tf_op jit(solution)/shard_map/transpose | solution.py:149
  15.9 1.2 dynamic-slice_bitcast_fusion.1
  17.0 8.8 %collective-permute-start = (bf16[4,4,128,256]{3,2,1,0:T(8,128)(2,1)}, bf16[4,4,128,256]{3,2,1,0:T(8,128)(2,1)S(1)}, u32[]{:S(2)}, u32[]{:S(2)}) collective-permute-start(bf16[4,4,128,256]{3,2,1,0:T(8,128)(2,1)} %get-tuple-element.20), channel_id=1, source_target_pairs={{0,32},{32,0},{64,96},{96,64},{128,160},{160,128},{192,224},{224,1... | collective-permute-start | bytes 3145736 | tf_op jit(solution)/shard_map/ppermute | solution.py:26
  25.8 3.5 %all-to-all-start = ((bf16[8,96,256]{2,1,0:T(8,128)(2,1)}), bf16[8,96,256]{2,1,0:T(8,128)(2,1)S(1)}, u32[]{:S(2)}, u32[]{:S(2)}) async-start(bf16[8,96,256]{2,1,0:T(8,128)(2,1)} %broadcast_in_dim.8), calls=%async_computation | async-start | bytes 786432 | tf_op jit(solution)/shard_map/all_to_all | solution.py:40
  29.4 1.0 copy-done.3
  30.3 1.5 pad_maximum_fusion
  31.8 12.6 %all-to-all-done = bf16[8,96,256]{2,1,0:T(8,128)(2,1)S(1)} async-done(((bf16[8,96,256]{2,1,0:T(8,128)(2,1)}), bf16[8,96,256]{2,1,0:T(8,128)(2,1)S(1)}, u32[]{:S(2)}, u32[]{:S(2)}) %all-to-all-start) | async-done | bytes 393248 | tf_op jit(solution)/shard_map/all_to_all | solution.py:40
  44.4 0.4 copy.13
  44.8 1.0 all_gather_reshape.3
  45.9 0.1 slice.52
  46.1 1.1 copy-done.2
  47.2 0.1 dynamic-slice_bitcast_fusion.4
  47.3 2.4 %collective-permute-start.7 = (bf16[3,2,128,256]{3,2,1,0:T(8,128)(2,1)S(1)}, bf16[3,2,128,256]{3,2,1,0:T(8,128)(2,1)}, u32[]{:S(2)}, u32[]{:S(2)}) collective-permute-start(bf16[3,2,128,256]{3,2,1,0:T(8,128)(2,1)S(1)} %get-tuple-element.25), channel_id=1, source_target_pairs={{0,192},{32,224},{64,0},{96,32},{128,64},{160,96},{192,128},{224,1... | collective-permute-start | bytes 1179656 | tf_op jit(solution)/shard_map/ppermute | solution.py:26
  49.8 2.4 %collective-permute-start.6 = (bf16[3,2,128,256]{3,2,1,0:T(8,128)(2,1)S(1)}, bf16[3,2,128,256]{3,2,1,0:T(8,128)(2,1)S(1)}, u32[]{:S(2)}, u32[]{:S(2)}) collective-permute-start(bf16[3,2,128,256]{3,2,1,0:T(8,128)(2,1)S(1)} %get-tuple-element.26), channel_id=1, source_target_pairs={{0,128},{32,160},{64,192},{96,224},{128,0},{160,32},{192,64},{224,... | collective-permute-start | bytes 1179656 | tf_op jit(solution)/shard_map/ppermute | solution.py:26
  52.2 0.9 fusion.8
  53.1 1.9 %collective-permute-start.1 = (bf16[4,2,128,256]{3,2,1,0:T(8,128)(2,1)S(1)}, bf16[4,2,128,256]{3,2,1,0:T(8,128)(2,1)}, u32[]{:S(2)}, u32[]{:S(2)}) collective-permute-start(bf16[4,2,128,256]{3,2,1,0:T(8,128)(2,1)S(1)} %get-tuple-element.18), channel_id=1, source_target_pairs={{0,256},{32,288},{64,320},{96,352},{128,384},{160,416},{192,448},{... | collective-permute-start | bytes 1572872 | tf_op jit(solution)/shard_map/ppermute | solution.py:26
  55.1 2.5 %collective-permute-start.5 = (bf16[3,2,128,256]{3,2,1,0:T(8,128)(2,1)S(1)}, bf16[3,2,128,256]{3,2,1,0:T(8,128)(2,1)S(1)}, u32[]{:S(2)}, u32[]{:S(2)}) collective-permute-start(bf16[3,2,128,256]{3,2,1,0:T(8,128)(2,1)S(1)} %get-tuple-element.24), channel_id=1, source_target_pairs={{0,64},{32,96},{64,128},{96,160},{128,192},{160,224},{192,0},{224,... | collective-permute-start | bytes 1179656 | tf_op jit(solution)/shard_map/ppermute | solution.py:26
  57.6 1.1 dynamic-slice_bitcast_fusion.7
  58.7 8.6 %collective-permute-done.7 = bf16[3,2,128,256]{3,2,1,0:T(8,128)(2,1)} collective-permute-done((bf16[3,2,128,256]{3,2,1,0:T(8,128)(2,1)S(1)}, bf16[3,2,128,256]{3,2,1,0:T(8,128)(2,1)}, u32[]{:S(2)}, u32[]{:S(2)}) %collective-permute-start.7) | collective-permute-done | bytes 393248 | tf_op jit(solution)/shard_map/ppermute | solution.py:26
  67.2 1.1 fusion.11
  68.3 8.1 %collective-permute-done.5 = bf16[3,2,128,256]{3,2,1,0:T(8,128)(2,1)S(1)} collective-permute-done((bf16[3,2,128,256]{3,2,1,0:T(8,128)(2,1)S(1)}, bf16[3,2,128,256]{3,2,1,0:T(8,128)(2,1)S(1)}, u32[]{:S(2)}, u32[]{:S(2)}) %collective-permute-start.5) | collective-permute-done | bytes 393248 | tf_op jit(solution)/shard_map/ppermute | solution.py:26
  76.4 0.1 pad_maximum_fusion.4.refs_0_
  76.5 7.1 %collective-permute-start.10 = (bf16[4,2,128,256]{3,2,1,0:T(8,128)(2,1)S(1)}, bf16[4,2,128,256]{3,2,1,0:T(8,128)(2,1)S(1)}, u32[]{:S(2)}, u32[]{:S(2)}) collective-permute-start(bf16[4,2,128,256]{3,2,1,0:T(8,128)(2,1)S(1)} %pad_maximum_fusion.4.refs_0_), channel_id=1, source_target_pairs={{0,256},{32,288},{64,320},{96,352},{128,384},{160,416},{192,448},{... | collective-permute-start | bytes 1572872 | tf_op jit(solution)/shard_map/ppermute | solution.py:26
  83.7 0.1 pad_maximum_fusion.3.refs_0_
  83.7 2.1 %collective-permute-start.9 = (bf16[4,2,128,256]{3,2,1,0:T(8,128)(2,1)S(1)}, bf16[4,2,128,256]{3,2,1,0:T(8,128)(2,1)S(1)}, u32[]{:S(2)}, u32[]{:S(2)}) collective-permute-start(bf16[4,2,128,256]{3,2,1,0:T(8,128)(2,1)S(1)} %pad_maximum_fusion.3.refs_0_), channel_id=1, source_target_pairs={{0,256},{32,288},{64,320},{96,352},{128,384},{160,416},{192,448},{... | collective-permute-start | bytes 1572872 | tf_op jit(solution)/shard_map/ppermute | solution.py:26
  85.8 0.1 pad_maximum_fusion.2.refs_0_
  85.9 7.1 %collective-permute-start.8 = (bf16[4,2,128,256]{3,2,1,0:T(8,128)(2,1)S(1)}, bf16[4,2,128,256]{3,2,1,0:T(8,128)(2,1)S(1)}, u32[]{:S(2)}, u32[]{:S(2)}) collective-permute-start(bf16[4,2,128,256]{3,2,1,0:T(8,128)(2,1)S(1)} %pad_maximum_fusion.2.refs_0_), channel_id=1, source_target_pairs={{0,256},{32,288},{64,320},{96,352},{128,384},{160,416},{192,448},{... | collective-permute-start | bytes 1572872 | tf_op jit(solution)/shard_map/ppermute | solution.py:26
  93.1 2.2 %fusion.1 = (bf16[2,2,128,256]{3,2,1,0:T(8,128)(2,1)}, bf16[2,2,128,256]{3,2,1,0:T(8,128)(2,1)}, bf16[2,2,128,256]{3,2,1,0:T(8,128)(2,1)}, bf16[2,2,128,256]{3,2,1,0:T(8,128)(2,1)S(1)}) fusion(s32[]{:T(128)S(6)} %select_n.79, bf16[4,1,2,128,256]{4,3,2,1,0:T(8,128)(2,1)} %get-tuple-element.17, bf16[4,1,2,128,256]{4,3,2,1,0:T(8,128)(2,1)} %bitcast.11, ...), kind=kLoop, calls=%fused_computation.19 | loop fusion | flops 524288 | bytes 2097168 | tf_op jit(solution)/shard_map/jit(dynamic_index_in_dim)/squeeze | solution.py:131
  95.3 2.5 %collective-permute-start.2 = (bf16[2,2,128,256]{3,2,1,0:T(8,128)(2,1)}, bf16[2,2,128,256]{3,2,1,0:T(8,128)(2,1)}, u32[]{:S(2)}, u32[]{:S(2)}) collective-permute-start(bf16[2,2,128,256]{3,2,1,0:T(8,128)(2,1)} %get-tuple-element.28), channel_id=1, source_target_pairs={{0,64},{32,96},{64,128},{96,160},{128,192},{160,224},{192,0},{224,... | collective-permute-start | bytes 786440 | tf_op jit(solution)/shard_map/ppermute | solution.py:26
  97.7 3.8 %collective-permute-start.3 = (bf16[2,2,128,256]{3,2,1,0:T(8,128)(2,1)}, bf16[2,2,128,256]{3,2,1,0:T(8,128)(2,1)}, u32[]{:S(2)}, u32[]{:S(2)}) collective-permute-start(bf16[2,2,128,256]{3,2,1,0:T(8,128)(2,1)} %get-tuple-element.29), channel_id=1, source_target_pairs={{0,128},{32,160},{64,192},{96,224},{128,0},{160,32},{192,64},{224,... | collective-permute-start | bytes 786440 | tf_op jit(solution)/shard_map/ppermute | solution.py:26
  101.5 0.3 collective-permute-done.10.refs_1_
  101.8 2.2 %collective-permute-start.4 = (bf16[2,2,128,256]{3,2,1,0:T(8,128)(2,1)}, bf16[2,2,128,256]{3,2,1,0:T(8,128)(2,1)}, u32[]{:S(2)}, u32[]{:S(2)}) collective-permute-start(bf16[2,2,128,256]{3,2,1,0:T(8,128)(2,1)} %get-tuple-element.27), channel_id=1, source_target_pairs={{0,192},{32,224},{64,0},{96,32},{128,64},{160,96},{192,128},{224,1... | collective-permute-start | bytes 786440 | tf_op jit(solution)/shard_map/ppermute | solution.py:26
  104.1 19.5 %all-gather.4.cloned.1.call-done.weight_ref = bf16[8,4,96,512]{3,2,1,0:T(8,128)(2,1)} async-done(((bf16[1,4,96,512]{3,2,1,0:T(8,128)(2,1)}), bf16[8,4,96,512]{3,2,1,0:T(8,128)(2,1)}) %all-gather.4.cloned.1.call-update) | async-done | bytes 3145744 | tf_op jit(solution)/shard_map/all_gather | solution.py:45
  123.5 2.8 %copy-done = bf16[1,1024,3072]{2,1,0:T(8,128)(2,1)S(1)} copy-done((bf16[1,1024,3072]{2,1,0:T(8,128)(2,1)S(1)}, bf16[1,1024,3072]{2,1,0:T(8,128)(2,1)}, u32[]{:S(2)}) %copy-start) | copy-done | bytes 6291480
  126.3 1.9 %copy-done.1 = bf16[8,4,96,512]{3,2,1,0:T(8,128)(2,1)S(1)} copy-done((bf16[8,4,96,512]{3,2,1,0:T(8,128)(2,1)S(1)}, bf16[8,4,96,512]{3,2,1,0:T(8,128)(2,1)}, u32[]{:S(2)}) %copy-start.1) | copy-done | bytes 3145752
  128.2 5.3 %shard_map.37 = bf16[4,1024,128]{2,1,0:T(8,128)(2,1)S(1)} custom-call(bf16[1024,3072]{1,0:T(8,128)(2,1)S(1)} %bitcast.52, bf16[8,4,96,512]{3,2,1,0:T(8,128)(2,1)S(1)} %copy-done.1), custom_call_target="tpu_custom_call" | custom-call | tf_op jit(solution)/shard_map/pallas_call | solution.py:69
  133.5 3.0 %shard_map.41 = bf16[8,128,128]{2,1,0:T(8,128)(2,1)S(1)} custom-call(bf16[4,8,128,128]{3,2,1,0:T(8,128)(2,1)S(1)} %bitcast.48, bf16[4,2,128,256]{3,2,1,0:T(8,128)(2,1)S(1)} %pad_maximum_fusion.4.refs_0_, bf16[4,2,128,256]{3,2,1,0:T(8,128)(2,1)S(1)} %collective-permute-done.10.refs_1_), custom_call_target="tpu_custom_call" | custom-call | tf_op jit(solution)/shard_map/pallas_call | solution.py:110
  136.5 3.0 %shard_map.40 = bf16[8,128,128]{2,1,0:T(8,128)(2,1)S(1)} custom-call(bf16[4,8,128,128]{3,2,1,0:T(8,128)(2,1)S(1)} %bitcast.49, bf16[4,2,128,256]{3,2,1,0:T(8,128)(2,1)S(1)} %pad_maximum_fusion.3.refs_0_, bf16[4,2,128,256]{3,2,1,0:T(8,128)(2,1)S(1)} %collective-permute-done.9.refs_1_), custom_call_target="tpu_custom_call" | custom-call | tf_op jit(solution)/shard_map/pallas_call | solution.py:110
  139.6 6.7 %collective-permute-done.8.refs_1_ = bf16[4,2,128,256]{3,2,1,0:T(8,128)(2,1)S(1)} collective-permute-done((bf16[4,2,128,256]{3,2,1,0:T(8,128)(2,1)S(1)}, bf16[4,2,128,256]{3,2,1,0:T(8,128)(2,1)S(1)}, u32[]{:S(2)}, u32[]{:S(2)}) %collective-permute-start.8) | collective-permute-done | bytes 524320 | tf_op jit(solution)/shard_map/ppermute | solution.py:26
  146.3 3.0 %shard_map.39 = bf16[8,128,128]{2,1,0:T(8,128)(2,1)S(1)} custom-call(bf16[4,8,128,128]{3,2,1,0:T(8,128)(2,1)S(1)} %bitcast.50, bf16[4,2,128,256]{3,2,1,0:T(8,128)(2,1)S(1)} %pad_maximum_fusion.2.refs_0_, bf16[4,2,128,256]{3,2,1,0:T(8,128)(2,1)S(1)} %collective-permute-done.8.refs_1_), custom_call_target="tpu_custom_call" | custom-call | tf_op jit(solution)/shard_map/pallas_call | solution.py:110
  149.4 4.1 %shard_map.38 = bf16[8,128,128]{2,1,0:T(8,128)(2,1)S(1)} custom-call(bf16[4,8,128,128]{3,2,1,0:T(8,128)(2,1)S(1)} %bitcast.51, bf16[2,2,128,256]{3,2,1,0:T(8,128)(2,1)S(1)} %get-tuple-element.30.refs_0_, bf16[2,2,128,256]{3,2,1,0:T(8,128)(2,1)} %collective-permute-done.2.refs_1_, bf16[2,2,128,256]{3,2,1,0:T(8,128)(2,1)} %collective-permute-done.3.refs_2_, ...), custom_call_target="tpu_custom_call" | custom-call | tf_op jit(solution)/shard_map/pallas_call | solution.py:110
  153.6 0.1 pad_maximum_fusion.1
  153.8 25.4 %all_to_all.10 = bf16[8,4,128,128]{3,2,1,0:T(8,128)(2,1)S(1)} all-to-all(bf16[8,4,128,128]{3,2,1,0:T(8,128)(2,1)S(1)} %copy.14), channel_id=1, replica_groups={{0,32,64,96,128,160,192,224},{256,288,320,352,384,416,448,480},{1,33,65..., dimensions={0} | all-to-all | bytes 2097152 | tf_op jit(solution)/shard_map/all_to_all | solution.py:31
  179.2 2.0 %copy.15 = bf16[128,2,8,2,128]{4,3,2,1,0:T(2,128)(2,1)} copy(bf16[128,2,8,2,128]{4,0,3,1,2:T(8,128)(2,1)S(1)} %bitcast.59) | data formatting | bytes 2097152 | tf_op jit(solution)/shard_map/transpose | solution.py:168
  (18 shorter events, 0.2 us)
Async XLA Ops:
  6.5 86.5 %all-gather.6.cloned.1.call-start = ((), (), s32[]{:S(2)}) async-start(), calls=%async_computation.3 | async-start | bytes 7077888 | tf_op jit(solution)/shard_map/all_gather | solution.py:144
  17.0 12.3 %collective-permute-start = (bf16[4,4,128,256]{3,2,1,0:T(8,128)(2,1)}, bf16[4,4,128,256]{3,2,1,0:T(8,128)(2,1)S(1)}, u32[]{:S(2)}, u32[]{:S(2)}) collective-permute-start(bf16[4,4,128,256]{3,2,1,0:T(8,128)(2,1)} %get-tuple-element.20), channel_id=1, source_target_pairs={{0,32},{32,0},{64,96},{96,64},{128,160},{160,128},{192,224},{224,1... | collective-permute-start | bytes 3145736 | tf_op jit(solution)/shard_map/ppermute | solution.py:26
  25.8 18.6 %all-to-all-start = ((bf16[8,96,256]{2,1,0:T(8,128)(2,1)}), bf16[8,96,256]{2,1,0:T(8,128)(2,1)S(1)}, u32[]{:S(2)}, u32[]{:S(2)}) async-start(bf16[8,96,256]{2,1,0:T(8,128)(2,1)} %broadcast_in_dim.8), calls=%async_computation | async-start | bytes 786432 | tf_op jit(solution)/shard_map/all_to_all | solution.py:40
  29.3 94.2 %all-gather.4.cloned.1.call-start = ((), (), s32[]{:S(2)}) async-start(), calls=%async_computation.2 | async-start | bytes 3538944 | tf_op jit(solution)/shard_map/all_gather | solution.py:45
  29.3 1.0 copy-start.3
  46.1 1.2 copy-start.2
  47.3 19.9 %collective-permute-start.7 = (bf16[3,2,128,256]{3,2,1,0:T(8,128)(2,1)S(1)}, bf16[3,2,128,256]{3,2,1,0:T(8,128)(2,1)}, u32[]{:S(2)}, u32[]{:S(2)}) collective-permute-start(bf16[3,2,128,256]{3,2,1,0:T(8,128)(2,1)S(1)} %get-tuple-element.25), channel_id=1, source_target_pairs={{0,192},{32,224},{64,0},{96,32},{128,64},{160,96},{192,128},{224,1... | collective-permute-start | bytes 1179656 | tf_op jit(solution)/shard_map/ppermute | solution.py:26
  49.8 18.5 %collective-permute-start.6 = (bf16[3,2,128,256]{3,2,1,0:T(8,128)(2,1)S(1)}, bf16[3,2,128,256]{3,2,1,0:T(8,128)(2,1)S(1)}, u32[]{:S(2)}, u32[]{:S(2)}) collective-permute-start(bf16[3,2,128,256]{3,2,1,0:T(8,128)(2,1)S(1)} %get-tuple-element.26), channel_id=1, source_target_pairs={{0,128},{32,160},{64,192},{96,224},{128,0},{160,32},{192,64},{224,... | collective-permute-start | bytes 1179656 | tf_op jit(solution)/shard_map/ppermute | solution.py:26
  53.1 39.9 %collective-permute-start.1 = (bf16[4,2,128,256]{3,2,1,0:T(8,128)(2,1)S(1)}, bf16[4,2,128,256]{3,2,1,0:T(8,128)(2,1)}, u32[]{:S(2)}, u32[]{:S(2)}) collective-permute-start(bf16[4,2,128,256]{3,2,1,0:T(8,128)(2,1)S(1)} %get-tuple-element.18), channel_id=1, source_target_pairs={{0,256},{32,288},{64,320},{96,352},{128,384},{160,416},{192,448},{... | collective-permute-start | bytes 1572872 | tf_op jit(solution)/shard_map/ppermute | solution.py:26
  55.1 21.3 %collective-permute-start.5 = (bf16[3,2,128,256]{3,2,1,0:T(8,128)(2,1)S(1)}, bf16[3,2,128,256]{3,2,1,0:T(8,128)(2,1)S(1)}, u32[]{:S(2)}, u32[]{:S(2)}) collective-permute-start(bf16[3,2,128,256]{3,2,1,0:T(8,128)(2,1)S(1)} %get-tuple-element.24), channel_id=1, source_target_pairs={{0,64},{32,96},{64,128},{96,160},{128,192},{160,224},{192,0},{224,... | collective-permute-start | bytes 1179656 | tf_op jit(solution)/shard_map/ppermute | solution.py:26
  76.5 25.3 %collective-permute-start.10 = (bf16[4,2,128,256]{3,2,1,0:T(8,128)(2,1)S(1)}, bf16[4,2,128,256]{3,2,1,0:T(8,128)(2,1)S(1)}, u32[]{:S(2)}, u32[]{:S(2)}) collective-permute-start(bf16[4,2,128,256]{3,2,1,0:T(8,128)(2,1)S(1)} %pad_maximum_fusion.4.refs_0_), channel_id=1, source_target_pairs={{0,256},{32,288},{64,320},{96,352},{128,384},{160,416},{192,448},{... | collective-permute-start | bytes 1572872 | tf_op jit(solution)/shard_map/ppermute | solution.py:26
  83.7 52.8 %collective-permute-start.9 = (bf16[4,2,128,256]{3,2,1,0:T(8,128)(2,1)S(1)}, bf16[4,2,128,256]{3,2,1,0:T(8,128)(2,1)S(1)}, u32[]{:S(2)}, u32[]{:S(2)}) collective-permute-start(bf16[4,2,128,256]{3,2,1,0:T(8,128)(2,1)S(1)} %pad_maximum_fusion.3.refs_0_), channel_id=1, source_target_pairs={{0,256},{32,288},{64,320},{96,352},{128,384},{160,416},{192,448},{... | collective-permute-start | bytes 1572872 | tf_op jit(solution)/shard_map/ppermute | solution.py:26
  85.9 60.5 %collective-permute-start.8 = (bf16[4,2,128,256]{3,2,1,0:T(8,128)(2,1)S(1)}, bf16[4,2,128,256]{3,2,1,0:T(8,128)(2,1)S(1)}, u32[]{:S(2)}, u32[]{:S(2)}) collective-permute-start(bf16[4,2,128,256]{3,2,1,0:T(8,128)(2,1)S(1)} %pad_maximum_fusion.2.refs_0_), channel_id=1, source_target_pairs={{0,256},{32,288},{64,320},{96,352},{128,384},{160,416},{192,448},{... | collective-permute-start | bytes 1572872 | tf_op jit(solution)/shard_map/ppermute | solution.py:26
  95.3 54.1 %collective-permute-start.2 = (bf16[2,2,128,256]{3,2,1,0:T(8,128)(2,1)}, bf16[2,2,128,256]{3,2,1,0:T(8,128)(2,1)}, u32[]{:S(2)}, u32[]{:S(2)}) collective-permute-start(bf16[2,2,128,256]{3,2,1,0:T(8,128)(2,1)} %get-tuple-element.28), channel_id=1, source_target_pairs={{0,64},{32,96},{64,128},{96,160},{128,192},{160,224},{192,0},{224,... | collective-permute-start | bytes 786440 | tf_op jit(solution)/shard_map/ppermute | solution.py:26
  97.7 51.7 %collective-permute-start.3 = (bf16[2,2,128,256]{3,2,1,0:T(8,128)(2,1)}, bf16[2,2,128,256]{3,2,1,0:T(8,128)(2,1)}, u32[]{:S(2)}, u32[]{:S(2)}) collective-permute-start(bf16[2,2,128,256]{3,2,1,0:T(8,128)(2,1)} %get-tuple-element.29), channel_id=1, source_target_pairs={{0,128},{32,160},{64,192},{96,224},{128,0},{160,32},{192,64},{224,... | collective-permute-start | bytes 786440 | tf_op jit(solution)/shard_map/ppermute | solution.py:26
  101.8 47.6 %collective-permute-start.4 = (bf16[2,2,128,256]{3,2,1,0:T(8,128)(2,1)}, bf16[2,2,128,256]{3,2,1,0:T(8,128)(2,1)}, u32[]{:S(2)}, u32[]{:S(2)}) collective-permute-start(bf16[2,2,128,256]{3,2,1,0:T(8,128)(2,1)} %get-tuple-element.27), channel_id=1, source_target_pairs={{0,192},{32,224},{64,0},{96,32},{128,64},{160,96},{192,128},{224,1... | collective-permute-start | bytes 786440 | tf_op jit(solution)/shard_map/ppermute | solution.py:26
  123.5 2.8 %copy-start = (bf16[1,1024,3072]{2,1,0:T(8,128)(2,1)S(1)}, bf16[1,1024,3072]{2,1,0:T(8,128)(2,1)}, u32[]{:S(2)}) copy-start(bf16[1,1024,3072]{2,1,0:T(8,128)(2,1)} %all-gather.6.cloned.1.call-done) | copy-start | bytes 18874372
  126.3 1.9 %copy-start.1 = (bf16[8,4,96,512]{3,2,1,0:T(8,128)(2,1)S(1)}, bf16[8,4,96,512]{3,2,1,0:T(8,128)(2,1)}, u32[]{:S(2)}) copy-start(bf16[8,4,96,512]{3,2,1,0:T(8,128)(2,1)} %all-gather.4.cloned.1.call-done.weight_ref) | copy-start | bytes 9437188
Sparse Core Ops, SparseCore 0:
  9.5 61.5 all-gather.5
  73.2 50.2 all-gather.3

commit v3 on v2

--- a/solution.py
+++ b/solution.py
@@ -117,22 +117,6 @@
     )(queries, *[part for part, _ in parts])
 
 
-def to_core(parts):
-    core = lax.axis_index("uly") % CORES
-    mine = lax.dynamic_index_in_dim(parts, core, 0, keepdims=False)
-    theirs = lax.dynamic_index_in_dim(parts, 1 - core, 0, keepdims=False)
-    return mine, send(theirs, 0, 0, 1)
-
-
-def to_column(parts):
-    x = lax.axis_index("uly") % GROUP // CORES
-    out = []
-    for dx in range(ALONG_X):
-        part = lax.dynamic_index_in_dim(parts, (x + dx) % ALONG_X, 0, keepdims=False)
-        out.append(send(part, 0, dx, 0) if dx else part)
-    return out
-
-
 def body(tokens, query_weight, key_values):
     rows, pair, width = query_weight.shape
     local_tokens, local_kv = tokens[0], key_values[0]
@@ -146,25 +130,22 @@
     copies, local_kv = together((copies, local_kv))
     block = spread_weight(copies)
 
-    spread = jnp.transpose(local_kv.reshape(token_count, HALVES, ALONG_X, CORES, pair, 2 * width), (3, 2, 1, 4, 0, 5))
-    spread = spread.reshape(CORES, ALONG_X, slots, token_count, 2 * width)
-    both = jnp.stack(to_core(spread), axis=2)
-    block, both = together((block, both))
-
-    lead = both[:, 0]
+    spread = jnp.transpose(local_kv.reshape(token_count, HALVES, GROUP, pair, 2 * width), (1, 2, 3, 0, 4))
+    block, lead, rest = together((block, spread[0], spread[1]))
     lead_far = send(lead, 1, 0, 0)
-    rest = to_column(both[:, 1:])
-    near = [jnp.stack([part[slot] for part in rest]) for slot in range(slots - 1)]
-    far = [send(keys, 1, 0, 0) for keys in near]
-    lead_far, gathered = together((lead_far, gathered))
-    early = to_column(jnp.stack([lead, lead_far], axis=1))
+    near = within_half(rest)
+    gathered, lead, lead_far, near = together((gathered, lead, lead_far, near))
+    far = [send(near[:, slot], 1, 0, 0) for slot in range(pair)]
+    early = within_half(jnp.stack([lead, lead_far], axis=1))
 
     block = jnp.transpose(block.reshape(HALVES, RUNS, rows, pair * width), (1, 2, 0, 3))
     weight = gather_ring(block.reshape(RUNS, rows, slots * width))
     queries = project(gathered, weight, slots).reshape(slots, GROUP, token_count, width)
-    outs = [attend(queries, 0, *[(part, None) for part in early])]
-    outs += [attend(queries, slot + 1, (near[slot], None), (far[slot], None)) for slot in range(slots - 1)]
-    heads = within_half(jnp.stack(outs, axis=1)).reshape(GROUP, HALVES, pair, token_count, width)
+    outs = [attend(queries, slot, (early, 2)) for slot in range(pair)]
+    outs += [attend(queries, pair + slot, (near, 1), (far[slot], None)) for slot in range(pair)]
+    first = within_half(jnp.stack(outs[:pair], axis=1))
+    first, last = together((first, outs[pair:]))
+    heads = jnp.stack([first, within_half(jnp.stack(last, axis=1))], axis=1)
     return jnp.transpose(heads, (3, 1, 0, 2, 4)).reshape(1, token_count, head_count, width)
 
 

time: 189 us -> 176 us (0.931)
  waiting for transfers between devices: 56.5 us -> 31.6 us
  blocking collectives: 25.4 us -> 47.3 us
  local copies, waits for them, and re-layouts: 23.4 us -> 16.6 us
  other arithmetic: 4.02 us -> 1.62 us
    ppermute x11 -> x3, starting transfers between devices: 42.9 us -> 12 us  [send(): return lax.ppermute(array, 'uly', pairs)]
    all_to_all x0 -> x2, starting transfers between devices: none -> 25.5 us  [within_half(): lax.all_to_all(array, 'uly', 0, 0, tiled=True, axis_index_groups=groups)]
    ppermute x11 -> x3, waiting for transfers between devices: 23.7 us -> 0.01 us  [send(): return lax.ppermute(array, 'uly', pairs)]
    all_to_all x1 -> x2, blocking collectives: 25.4 us -> 47.3 us  [within_half(): lax.all_to_all(array, 'uly', 0, 0, tiled=True, axis_index_groups=groups)]
    transpose x2 -> x0, local copies, waits for them, and re-layouts: 4.81 us -> none  [the longest x1 2.76 us: body(): jnp.transpose(local_kv.reshape(token_count, HALVES, ALONG_X, CORES, pair,...]
    all_to_all x1, starting transfers between devices: 3.46 us -> 7.65 us  [spread_weight(): lax.all_to_all(copies, ('uly', 'blk'), 0, 0, tiled=True, axis_index_group...]
    all_gather x1, waiting for transfers between devices: 19.5 us -> 15.8 us  [gather_ring(): return lax.all_gather(block, 'blk', axis=0, axis_index_groups=rings)]
    all_gather x1, waiting for transfers between devices: 0.02 us -> 3.28 us  [body(): lax.all_gather(local_tokens, 'uly', axis=0, tiled=True, axis_index_groups...]
  transfers between devices with their start and end apart: 14 -> 8, of which waited for: 6 -> 4; matrix products, arithmetic and copies ran while one was open for 10% -> 7% of each run, Pallas kernels for 8% -> 11%
where the time goes in v3:
time: 176 us; the launch traced here: 175 us
  blocking collectives  47.3 us (27%)
  starting transfers between devices  45.1 us (26%)
  waiting for transfers between devices  31.6 us (18%)
  Pallas kernels  19.3 us (11%)
  local copies, waits for them, and re-layouts  16.6 us (9%)
  between operations  13.5 us (8%)
    all_to_all x2, blocking collectives, within_half(): lax.all_to_all(array, 'uly', 0, 0, tiled=True, axis_index_groups=groups)  47.3 us
    all_to_all x2, starting transfers between devices, within_half(): lax.all_to_all(array, 'uly', 0, 0, tiled=True, axis_index_groups=groups)  25.5 us
    all_gather x1, waiting for transfers between devices, gather_ring(): return lax.all_gather(block, 'blk', axis=0, axis_index_groups=rings)  15.8 us
    pallas_call x4, Pallas kernels, attend(): pl.pallas_call(attend_kernel, out_shape=jax.ShapeDtypeStruct((members, ro...  14.2 us
    ppermute x3, starting transfers between devices, send(): return lax.ppermute(array, 'uly', pairs)  12 us
    all_to_all x1, waiting for transfers between devices, spread_weight(): lax.all_to_all(copies, ('uly', 'blk'), 0, 0, tiled=True, axis_index_group...  10.4 us
    unnamed x12, local copies, waits for them, and re-layouts  8.26 us
    all_to_all x1, starting transfers between devices, spread_weight(): lax.all_to_all(copies, ('uly', 'blk'), 0, 0, tiled=True, axis_index_group...  7.65 us
  transfers between devices with their start and end apart: 8, of which 4 were waited for; matrix products, arithmetic and copies ran while one was open for 7% of the time, Pallas kernels for 11%

profile of v3, /device:TPU:1, one launch (start us, length us, event | category | flops | bytes accessed | tf_op | source)
XLA Modules:
  0.0 175.1 jit_solution(17297667145027783776)
XLA Ops:
  6.5 0.0 all-gather.6.cloned.1.call-start
  6.5 0.7 all-gather.6.cloned.1.call-update
  7.3 0.8 copy.38
  8.1 2.8 %copy.37 = bf16[1,128,32,256]{3,1,2,0:T(8,128)(2,1)S(1)} copy(bf16[1,128,32,256]{3,2,1,0:T(8,128)(2,1)} %param.5) | data formatting | bytes 4194304 | tf_op args[2]
  10.8 0.8 broadcast_in_dim.8
  11.6 7.7 %all-to-all-start = ((bf16[8,96,256]{2,1,0:T(8,128)(2,1)}), bf16[8,96,256]{2,1,0:T(8,128)(2,1)S(1)}, u32[]{:S(2)}, u32[]{:S(2)}) async-start(bf16[8,96,256]{2,1,0:T(8,128)(2,1)} %broadcast_in_dim.8), calls=%async_computation | async-start | bytes 786432 | tf_op jit(solution)/shard_map/all_to_all | solution.py:40
  19.3 0.0 all-gather.4.cloned.1.call-start
  19.3 1.2 slice_bitcast_fusion
  20.5 0.0 copy-start.4
  20.5 10.4 %all-to-all-done = bf16[8,96,256]{2,1,0:T(8,128)(2,1)S(1)} async-done(((bf16[8,96,256]{2,1,0:T(8,128)(2,1)}), bf16[8,96,256]{2,1,0:T(8,128)(2,1)S(1)}, u32[]{:S(2)}, u32[]{:S(2)}) %all-to-all-start) | async-done | bytes 393248 | tf_op jit(solution)/shard_map/all_to_all | solution.py:40
  30.9 0.4 copy.25
  31.3 1.0 all_gather_reshape.3
  32.3 0.0 all-gather.4.cloned.1.call-update
  32.3 2.8 %collective-permute-start = (bf16[8,2,128,256]{3,2,1,0:T(8,128)(2,1)}, bf16[8,2,128,256]{3,2,1,0:T(8,128)(2,1)}, u32[]{:S(2)}, u32[]{:S(2)}) collective-permute-start(bf16[8,2,128,256]{3,2,1,0:T(8,128)(2,1)} %get-tuple-element.23), channel_id=1, source_target_pairs={{0,256},{32,288},{64,320},{96,352},{128,384},{160,416},{192,448},{... | collective-permute-start | bytes 3145736 | tf_op jit(solution)/shard_map/ppermute | solution.py:26
  35.1 34.5 %all_to_all.25.refs_0_ = bf16[8,2,128,256]{3,2,1,0:T(8,128)(2,1)S(1)} all-to-all(bf16[8,2,128,256]{3,2,1,0:T(8,128)(2,1)S(1)} %get-tuple-element.20), channel_id=1, replica_groups={{0,32,64,96,128,160,192,224},{256,288,320,352,384,416,448,480},{1,33,65..., dimensions={0} | all-to-all | bytes 2097152 | tf_op jit(solution)/shard_map/all_to_all | solution.py:31
  69.6 0.0 copy-start
  69.6 0.0 collective-permute-done
  69.6 3.3 %all-gather.6.cloned.1.call-done = bf16[1,1024,3072]{2,1,0:T(8,128)(2,1)} async-done(((bf16[1,128,3072]{2,1,0:T(8,128)(2,1)}), bf16[1,1024,3072]{2,1,0:T(8,128)(2,1)}) %all-gather.6.cloned.1.call-update) | async-done | bytes 6291472 | tf_op jit(solution)/shard_map/all_gather | solution.py:128
  72.9 0.0 copy-done.4
  72.9 1.4 pad_maximum_fusion
  74.3 1.4 copy.26
  75.7 20.6 %all-to-all-start.2 = ((bf16[8,2,2,128,256]{4,3,2,1,0:T(8,128)(2,1)}), bf16[8,2,2,128,256]{4,3,2,1,0:T(8,128)(2,1)S(1)}, u32[]{:S(2)}, u32[]{:S(2)}) async-start(bf16[8,2,2,128,256]{4,3,2,1,0:T(8,128)(2,1)} %copy.26), calls=%async_computation.2 | async-start | bytes 4194304 | tf_op jit(solution)/shard_map/all_to_all | solution.py:31
  96.3 0.0 copy-done
  96.3 1.1 slice_bitcast_fusion.2
  97.4 2.1 %collective-permute-start.2 = (bf16[8,128,256]{2,1,0:T(8,128)(2,1)}, bf16[8,128,256]{2,1,0:T(8,128)(2,1)}, u32[]{:S(2)}, u32[]{:S(2)}) collective-permute-start(bf16[8,128,256]{2,1,0:T(8,128)(2,1)} %get-tuple-element.31), channel_id=1, source_target_pairs={{0,256},{32,288},{64,320},{96,352},{128,384},{160,416},{192,448},{... | collective-permute-start | bytes 1572872 | tf_op jit(solution)/shard_map/ppermute | solution.py:26
  99.5 7.1 %collective-permute-start.1 = (bf16[8,128,256]{2,1,0:T(8,128)(2,1)}, bf16[8,128,256]{2,1,0:T(8,128)(2,1)}, u32[]{:S(2)}, u32[]{:S(2)}) collective-permute-start(bf16[8,128,256]{2,1,0:T(8,128)(2,1)} %get-tuple-element.32), channel_id=1, source_target_pairs={{0,256},{32,288},{64,320},{96,352},{128,384},{160,416},{192,448},{... | collective-permute-start | bytes 1572872 | tf_op jit(solution)/shard_map/ppermute | solution.py:26
  106.6 15.8 %all-gather.4.cloned.1.call-done.weight_ref = bf16[8,4,96,512]{3,2,1,0:T(8,128)(2,1)} async-done(((bf16[1,4,96,512]{3,2,1,0:T(8,128)(2,1)}), bf16[8,4,96,512]{3,2,1,0:T(8,128)(2,1)}) %all-gather.4.cloned.1.call-update) | async-done | bytes 3145744 | tf_op jit(solution)/shard_map/all_gather | solution.py:45
  122.5 0.0 copy-start.2
  122.5 2.8 %copy-done.2 = bf16[1,1024,3072]{2,1,0:T(8,128)(2,1)S(1)} copy-done((bf16[1,1024,3072]{2,1,0:T(8,128)(2,1)S(1)}, bf16[1,1024,3072]{2,1,0:T(8,128)(2,1)}, u32[]{:S(2)}) %copy-start.2) | copy-done | bytes 6291480
  125.3 1.9 %copy-done.3 = bf16[8,4,96,512]{3,2,1,0:T(8,128)(2,1)S(1)} copy-done((bf16[8,4,96,512]{3,2,1,0:T(8,128)(2,1)S(1)}, bf16[8,4,96,512]{3,2,1,0:T(8,128)(2,1)}, u32[]{:S(2)}) %copy-start.3) | copy-done | bytes 3145752
  127.1 5.1 %shard_map.37 = bf16[4,1024,128]{2,1,0:T(8,128)(2,1)S(1)} custom-call(bf16[1024,3072]{1,0:T(8,128)(2,1)S(1)} %bitcast.38, bf16[8,4,96,512]{3,2,1,0:T(8,128)(2,1)S(1)} %copy-done.3), custom_call_target="tpu_custom_call" | custom-call | tf_op jit(solution)/shard_map/pallas_call | solution.py:69
  132.2 0.0 all-to-all-done.2.refs_0_
  132.2 3.0 %shard_map.39 = bf16[8,128,128]{2,1,0:T(8,128)(2,1)S(1)} custom-call(bf16[4,8,128,128]{3,2,1,0:T(8,128)(2,1)S(1)} %bitcast.34, bf16[8,2,2,128,256]{4,3,2,1,0:T(8,128)(2,1)S(1)} %all-to-all-done.2.refs_0_), custom_call_target="tpu_custom_call" | custom-call | tf_op jit(solution)/shard_map/pallas_call | solution.py:110
  135.3 3.0 %shard_map.38 = bf16[8,128,128]{2,1,0:T(8,128)(2,1)S(1)} custom-call(bf16[4,8,128,128]{3,2,1,0:T(8,128)(2,1)S(1)} %bitcast.35, bf16[8,2,2,128,256]{4,3,2,1,0:T(8,128)(2,1)S(1)} %all-to-all-done.2.refs_0_), custom_call_target="tpu_custom_call" | custom-call | tf_op jit(solution)/shard_map/pallas_call | solution.py:110
  138.3 0.0 copy-start.1
  138.3 0.1 pad_maximum_fusion.2
  138.4 0.8 copy.27
  139.2 4.9 %all-to-all-start.3 = ((bf16[8,2,128,128]{3,2,1,0:T(8,128)(2,1)}), bf16[8,2,128,128]{3,2,1,0:T(8,128)(2,1)S(1)}, u32[]{:S(2)}, u32[]{:S(2)}) async-start(bf16[8,2,128,128]{3,2,1,0:T(8,128)(2,1)} %copy.27), calls=%async_computation.3 | async-start | bytes 1048576 | tf_op jit(solution)/shard_map/all_to_all | solution.py:31
  144.1 0.0 collective-permute-done.2.refs_1_
  144.1 0.0 copy-done.1
  144.1 4.1 %shard_map.41 = bf16[8,128,128]{2,1,0:T(8,128)(2,1)S(1)} custom-call(bf16[4,8,128,128]{3,2,1,0:T(8,128)(2,1)S(1)} %bitcast.36, bf16[8,2,128,256]{3,2,1,0:T(8,128)(2,1)S(1)} %copy-done.1, bf16[8,128,256]{2,1,0:T(8,128)(2,1)} %collective-permute-done.2.refs_1_), custom_call_target="tpu_custom_call" | custom-call | tf_op jit(solution)/shard_map/pallas_call | solution.py:110
  148.2 0.0 collective-permute-done.1.refs_1_
  148.2 4.1 %shard_map.40 = bf16[8,128,128]{2,1,0:T(8,128)(2,1)S(1)} custom-call(bf16[4,8,128,128]{3,2,1,0:T(8,128)(2,1)S(1)} %bitcast.37, bf16[8,2,128,256]{3,2,1,0:T(8,128)(2,1)S(1)} %copy-done.1, bf16[8,128,256]{2,1,0:T(8,128)(2,1)} %collective-permute-done.1.refs_1_), custom_call_target="tpu_custom_call" | custom-call | tf_op jit(solution)/shard_map/pallas_call | solution.py:110
  152.3 1.3 all-to-all-done.3
  153.6 0.1 pad_maximum_fusion.3
  153.7 12.8 %all_to_all.26 = bf16[8,2,128,128]{3,2,1,0:T(8,128)(2,1)S(1)} all-to-all(bf16[8,2,128,128]{3,2,1,0:T(8,128)(2,1)S(1)} %copy.30), channel_id=1, replica_groups={{0,32,64,96,128,160,192,224},{256,288,320,352,384,416,448,480},{1,33,65..., dimensions={0} | all-to-all | bytes 1048576 | tf_op jit(solution)/shard_map/all_to_all | solution.py:31
  166.5 0.1 pad_maximum_fusion.1
  166.6 1.6 copy.31
  (2 shorter events, 0.0 us)
Async XLA Ops:
  6.5 66.4 %all-gather.6.cloned.1.call-start = ((), (), s32[]{:S(2)}) async-start(), calls=%async_computation.6 | async-start | bytes 7077888 | tf_op jit(solution)/shard_map/all_gather | solution.py:128
  11.6 19.3 %all-to-all-start = ((bf16[8,96,256]{2,1,0:T(8,128)(2,1)}), bf16[8,96,256]{2,1,0:T(8,128)(2,1)S(1)}, u32[]{:S(2)}, u32[]{:S(2)}) async-start(bf16[8,96,256]{2,1,0:T(8,128)(2,1)} %broadcast_in_dim.8), calls=%async_computation | async-start | bytes 786432 | tf_op jit(solution)/shard_map/all_to_all | solution.py:40
  19.3 103.2 %all-gather.4.cloned.1.call-start = ((), (), s32[]{:S(2)}) async-start(), calls=%async_computation.5 | async-start | bytes 3538944 | tf_op jit(solution)/shard_map/all_gather | solution.py:45
  20.5 52.4 %copy-start.4 = (bf16[8,2,128,256]{3,2,1,0:T(8,128)(2,1)S(1)}, bf16[8,2,128,256]{3,2,1,0:T(8,128)(2,1)}, u32[]{:S(2)}) copy-start(bf16[8,2,128,256]{3,2,1,0:T(8,128)(2,1)} %get-tuple-element.23) | copy-start | bytes 3145732
  32.3 37.3 %collective-permute-start = (bf16[8,2,128,256]{3,2,1,0:T(8,128)(2,1)}, bf16[8,2,128,256]{3,2,1,0:T(8,128)(2,1)}, u32[]{:S(2)}, u32[]{:S(2)}) collective-permute-start(bf16[8,2,128,256]{3,2,1,0:T(8,128)(2,1)} %get-tuple-element.23), channel_id=1, source_target_pairs={{0,256},{32,288},{64,320},{96,352},{128,384},{160,416},{192,448},{... | collective-permute-start | bytes 3145736 | tf_op jit(solution)/shard_map/ppermute | solution.py:26
  69.6 26.7 %copy-start = (bf16[8,2,128,256]{3,2,1,0:T(8,128)(2,1)}, bf16[8,2,128,256]{3,2,1,0:T(8,128)(2,1)S(1)}, u32[]{:S(2)}) copy-start(bf16[8,2,128,256]{3,2,1,0:T(8,128)(2,1)S(1)} %all_to_all.25.refs_0_) | copy-start | bytes 3145732
  75.7 56.5 %all-to-all-start.2 = ((bf16[8,2,2,128,256]{4,3,2,1,0:T(8,128)(2,1)}), bf16[8,2,2,128,256]{4,3,2,1,0:T(8,128)(2,1)S(1)}, u32[]{:S(2)}, u32[]{:S(2)}) async-start(bf16[8,2,2,128,256]{4,3,2,1,0:T(8,128)(2,1)} %copy.26), calls=%async_computation.2 | async-start | bytes 4194304 | tf_op jit(solution)/shard_map/all_to_all | solution.py:31
  97.4 46.7 %collective-permute-start.2 = (bf16[8,128,256]{2,1,0:T(8,128)(2,1)}, bf16[8,128,256]{2,1,0:T(8,128)(2,1)}, u32[]{:S(2)}, u32[]{:S(2)}) collective-permute-start(bf16[8,128,256]{2,1,0:T(8,128)(2,1)} %get-tuple-element.31), channel_id=1, source_target_pairs={{0,256},{32,288},{64,320},{96,352},{128,384},{160,416},{192,448},{... | collective-permute-start | bytes 1572872 | tf_op jit(solution)/shard_map/ppermute | solution.py:26
  99.5 48.7 %collective-permute-start.1 = (bf16[8,128,256]{2,1,0:T(8,128)(2,1)}, bf16[8,128,256]{2,1,0:T(8,128)(2,1)}, u32[]{:S(2)}, u32[]{:S(2)}) collective-permute-start(bf16[8,128,256]{2,1,0:T(8,128)(2,1)} %get-tuple-element.32), channel_id=1, source_target_pairs={{0,256},{32,288},{64,320},{96,352},{128,384},{160,416},{192,448},{... | collective-permute-start | bytes 1572872 | tf_op jit(solution)/shard_map/ppermute | solution.py:26
  122.5 2.8 %copy-start.2 = (bf16[1,1024,3072]{2,1,0:T(8,128)(2,1)S(1)}, bf16[1,1024,3072]{2,1,0:T(8,128)(2,1)}, u32[]{:S(2)}) copy-start(bf16[1,1024,3072]{2,1,0:T(8,128)(2,1)} %all-gather.6.cloned.1.call-done) | copy-start | bytes 18874372
  125.3 1.9 %copy-start.3 = (bf16[8,4,96,512]{3,2,1,0:T(8,128)(2,1)S(1)}, bf16[8,4,96,512]{3,2,1,0:T(8,128)(2,1)}, u32[]{:S(2)}) copy-start(bf16[8,4,96,512]{3,2,1,0:T(8,128)(2,1)} %all-gather.4.cloned.1.call-done.weight_ref) | copy-start | bytes 9437188
  138.3 5.8 %copy-start.1 = (bf16[8,2,128,256]{3,2,1,0:T(8,128)(2,1)S(1)}, bf16[8,2,128,256]{3,2,1,0:T(8,128)(2,1)}, u32[]{:S(2)}) copy-start(bf16[8,2,128,256]{3,2,1,0:T(8,128)(2,1)} %copy-done) | copy-start | bytes 3145732
  139.2 14.4 %all-to-all-start.3 = ((bf16[8,2,128,128]{3,2,1,0:T(8,128)(2,1)}), bf16[8,2,128,128]{3,2,1,0:T(8,128)(2,1)S(1)}, u32[]{:S(2)}, u32[]{:S(2)}) async-start(bf16[8,2,128,128]{3,2,1,0:T(8,128)(2,1)} %copy.27), calls=%async_computation.3 | async-start | bytes 1048576 | tf_op jit(solution)/shard_map/all_to_all | solution.py:31
Sparse Core Ops, SparseCore 0:
  9.5 63.3 all-gather.5
  75.0 47.4 all-gather.3

commit v4 on v3

--- a/solution.py
+++ b/solution.py
@@ -65,7 +65,7 @@
     count, depth = tokens.shape
     columns = weight.shape[-1]
     width = columns // slots
-    block = 128
+    block = min(512, count)
     return pl.pallas_call(
         project_kernel,
         out_shape=jax.ShapeDtypeStruct((slots, count, width), tokens.dtype),
@@ -76,7 +76,7 @@
         ],
         out_specs=pl.BlockSpec((slots, block, width), lambda i: (0, i, 0)),
         scratch_shapes=[pltpu.VMEM((depth, columns), weight.dtype)],
-        compiler_params=pltpu.CompilerParams(vmem_limit_bytes=32 * 2**20),
+        compiler_params=pltpu.CompilerParams(vmem_limit_bytes=56 * 2**20),
     )(tokens, weight)
 
 
@@ -134,9 +134,10 @@
     block, lead, rest = together((block, spread[0], spread[1]))
     lead_far = send(lead, 1, 0, 0)
     near = within_half(rest)
-    gathered, lead, lead_far, near = together((gathered, lead, lead_far, near))
+    early = jnp.stack([lead, lead_far], axis=1)
+    gathered, early, near = together((gathered, early, near))
     far = [send(near[:, slot], 1, 0, 0) for slot in range(pair)]
-    early = within_half(jnp.stack([lead, lead_far], axis=1))
+    early = within_half(early)
 
     block = jnp.transpose(block.reshape(HALVES, RUNS, rows, pair * width), (1, 2, 0, 3))
     weight = gather_ring(block.reshape(RUNS, rows, slots * width))

time: 176 us -> 175 us (level)
  blocking collectives: 47.3 us -> 12.8 us
  waiting for transfers between devices: 31.6 us -> 58.1 us
  starting transfers between devices: 45.1 us -> 54.1 us
  local copies, waits for them, and re-layouts: 16.6 us -> 12.4 us
  Pallas kernels: 19.3 us -> 21.7 us
    all_to_all x2 -> x1, blocking collectives: 47.3 us -> 12.8 us  [within_half(): lax.all_to_all(array, 'uly', 0, 0, tiled=True, axis_index_groups=groups)]
    ppermute x3, waiting for transfers between devices: 0.01 us -> 24.1 us  [send(): return lax.ppermute(array, 'uly', pairs)]
    all_to_all x2 -> x3, starting transfers between devices: 25.5 us -> 34.4 us  [within_half(): lax.all_to_all(array, 'uly', 0, 0, tiled=True, axis_index_groups=groups)]
    unnamed x12 -> x10, local copies, waits for them, and re-layouts: 8.26 us -> 4.03 us
    pallas_call x1, Pallas kernels: 5.09 us -> 7.44 us  [project(): pl.pallas_call(project_kernel, out_shape=jax.ShapeDtypeStruct((slots, cou...]
  transfers between devices with their start and end apart: 8 -> 9, of which waited for: 4 -> 6; matrix products, arithmetic and copies ran while one was open for 7% -> 6% of each run, Pallas kernels for 11% -> 12%
where the time goes in v4:
time: 175 us
  waiting for transfers between devices  58.1 us (33%)
  starting transfers between devices  54.1 us (31%)
  Pallas kernels  21.7 us (12%)
  between operations  13.5 us (8%)
  blocking collectives  12.8 us (7%)
  local copies, waits for them, and re-layouts  12.4 us (7%)
  other arithmetic  1.93 us (1%)
    all_to_all x3, starting transfers between devices, within_half(): lax.all_to_all(array, 'uly', 0, 0, tiled=True, axis_index_groups=groups)  34.4 us
    ppermute x3, waiting for transfers between devices, send(): return lax.ppermute(array, 'uly', pairs)  24.1 us
    all_gather x1, waiting for transfers between devices, gather_ring(): return lax.all_gather(block, 'blk', axis=0, axis_index_groups=rings)  16.9 us
    pallas_call x4, Pallas kernels, attend(): pl.pallas_call(attend_kernel, out_shape=jax.ShapeDtypeStruct((members, ro...  14.2 us
    all_to_all x1, blocking collectives, within_half(): lax.all_to_all(array, 'uly', 0, 0, tiled=True, axis_index_groups=groups)  12.8 us
    ppermute x3, starting transfers between devices, send(): return lax.ppermute(array, 'uly', pairs)  12 us
    all_to_all x1, waiting for transfers between devices, spread_weight(): lax.all_to_all(copies, ('uly', 'blk'), 0, 0, tiled=True, axis_index_group...  10.4 us
    all_to_all x1, starting transfers between devices, spread_weight(): lax.all_to_all(copies, ('uly', 'blk'), 0, 0, tiled=True, axis_index_group...  7.65 us
  transfers between devices with their start and end apart: 9, of which 6 were waited for; matrix products, arithmetic and copies ran while one was open for 6% of the time, Pallas kernels for 12%

profile of v4, /device:TPU:1, one launch (start us, length us, event | category | flops | bytes accessed | tf_op | source)
XLA Modules:
  0.0 174.6 jit_solution(16432935936059427140)
XLA Ops:
  6.5 0.0 all-gather.6.cloned.1.call-start
  6.5 0.7 all-gather.6.cloned.1.call-update
  7.3 0.0 copy-start.3
  7.3 2.8 %copy.37 = bf16[1,128,32,256]{3,1,2,0:T(8,128)(2,1)S(1)} copy(bf16[1,128,32,256]{3,2,1,0:T(8,128)(2,1)} %param.5) | data formatting | bytes 4194304 | tf_op args[2]
  10.0 0.0 copy-done.3
  10.1 0.8 broadcast_in_dim.8
  10.8 7.7 %all-to-all-start = ((bf16[8,96,256]{2,1,0:T(8,128)(2,1)}), bf16[8,96,256]{2,1,0:T(8,128)(2,1)S(1)}, u32[]{:S(2)}, u32[]{:S(2)}) async-start(bf16[8,96,256]{2,1,0:T(8,128)(2,1)} %broadcast_in_dim.8), calls=%async_computation | async-start | bytes 786432 | tf_op jit(solution)/shard_map/all_to_all | solution.py:40
  18.5 0.0 all-gather.4.cloned.1.call-start
  18.5 1.2 slice_bitcast_fusion
  19.7 0.0 copy-start.2
  19.7 10.4 %all-to-all-done = bf16[8,96,256]{2,1,0:T(8,128)(2,1)S(1)} async-done(((bf16[8,96,256]{2,1,0:T(8,128)(2,1)}), bf16[8,96,256]{2,1,0:T(8,128)(2,1)S(1)}, u32[]{:S(2)}, u32[]{:S(2)}) %all-to-all-start) | async-done | bytes 393248 | tf_op jit(solution)/shard_map/all_to_all | solution.py:40
  30.1 0.4 copy.25
  30.5 1.0 all_gather_reshape.3
  31.5 0.0 all-gather.4.cloned.1.call-update
  31.6 2.8 %collective-permute-start = (bf16[8,2,128,256]{3,2,1,0:T(8,128)(2,1)S(1)}, bf16[8,2,128,256]{3,2,1,0:T(8,128)(2,1)}, u32[]{:S(2)}, u32[]{:S(2)}) collective-permute-start(bf16[8,2,128,256]{3,2,1,0:T(8,128)(2,1)S(1)} %get-tuple-element.18), channel_id=1, source_target_pairs={{0,256},{32,288},{64,320},{96,352},{128,384},{160,416},{192,448},{... | collective-permute-start | bytes 3145736 | tf_op jit(solution)/shard_map/ppermute | solution.py:26
  34.4 8.0 %all-to-all-start.1 = ((bf16[8,2,128,256]{3,2,1,0:T(8,128)(2,1)}), bf16[8,2,128,256]{3,2,1,0:T(8,128)(2,1)S(1)}, u32[]{:S(2)}, u32[]{:S(2)}) async-start(bf16[8,2,128,256]{3,2,1,0:T(8,128)(2,1)} %get-tuple-element.19), calls=%async_computation.1 | async-start | bytes 2097152 | tf_op jit(solution)/shard_map/all_to_all | solution.py:31
  42.4 24.0 %collective-permute-done = bf16[8,2,128,256]{3,2,1,0:T(8,128)(2,1)} collective-permute-done((bf16[8,2,128,256]{3,2,1,0:T(8,128)(2,1)S(1)}, bf16[8,2,128,256]{3,2,1,0:T(8,128)(2,1)}, u32[]{:S(2)}, u32[]{:S(2)}) %collective-permute-start) | collective-permute-done | bytes 1048608 | tf_op jit(solution)/shard_map/ppermute | solution.py:26
  66.4 0.0 copy-done.2
  66.4 1.7 pad_maximum_fusion
  68.2 0.9 all-to-all-done.1.refs_0_
  69.1 3.8 %all-gather.6.cloned.1.call-done = bf16[1,1024,3072]{2,1,0:T(8,128)(2,1)} async-done(((bf16[1,128,3072]{2,1,0:T(8,128)(2,1)}), bf16[1,1024,3072]{2,1,0:T(8,128)(2,1)}) %all-gather.6.cloned.1.call-update) | async-done | bytes 6291472 | tf_op jit(solution)/shard_map/all_gather | solution.py:128
  72.9 1.4 copy.26
  74.3 21.5 %all-to-all-start.2 = ((bf16[8,2,2,128,256]{4,3,2,1,0:T(8,128)(2,1)}), bf16[8,2,2,128,256]{4,3,2,1,0:T(8,128)(2,1)S(1)}, u32[]{:S(2)}, u32[]{:S(2)}) async-start(bf16[8,2,2,128,256]{4,3,2,1,0:T(8,128)(2,1)} %copy.26), calls=%async_computation.2 | async-start | bytes 4194304 | tf_op jit(solution)/shard_map/all_to_all | solution.py:31
  95.9 1.1 slice_bitcast_fusion.2
  96.9 2.0 %collective-permute-start.2 = (bf16[8,128,256]{2,1,0:T(8,128)(2,1)}, bf16[8,128,256]{2,1,0:T(8,128)(2,1)}, u32[]{:S(2)}, u32[]{:S(2)}) collective-permute-start(bf16[8,128,256]{2,1,0:T(8,128)(2,1)} %get-tuple-element.29), channel_id=1, source_target_pairs={{0,256},{32,288},{64,320},{96,352},{128,384},{160,416},{192,448},{... | collective-permute-start | bytes 1572872 | tf_op jit(solution)/shard_map/ppermute | solution.py:26
  98.9 7.2 %collective-permute-start.1 = (bf16[8,128,256]{2,1,0:T(8,128)(2,1)}, bf16[8,128,256]{2,1,0:T(8,128)(2,1)}, u32[]{:S(2)}, u32[]{:S(2)}) collective-permute-start(bf16[8,128,256]{2,1,0:T(8,128)(2,1)} %get-tuple-element.30), channel_id=1, source_target_pairs={{0,256},{32,288},{64,320},{96,352},{128,384},{160,416},{192,448},{... | collective-permute-start | bytes 1572872 | tf_op jit(solution)/shard_map/ppermute | solution.py:26
  106.1 16.9 %all-gather.4.cloned.1.call-done.weight_ref = bf16[8,4,96,512]{3,2,1,0:T(8,128)(2,1)} async-done(((bf16[1,4,96,512]{3,2,1,0:T(8,128)(2,1)}), bf16[8,4,96,512]{3,2,1,0:T(8,128)(2,1)}) %all-gather.4.cloned.1.call-update) | async-done | bytes 3145744 | tf_op jit(solution)/shard_map/all_gather | solution.py:45
  123.0 7.4 %shard_map.37 = bf16[4,1024,128]{2,1,0:T(8,128)(2,1)} custom-call(bf16[1024,3072]{1,0:T(8,128)(2,1)} %bitcast.43, bf16[8,4,96,512]{3,2,1,0:T(8,128)(2,1)} %all-gather.4.cloned.1.call-done.weight_ref), custom_call_target="tpu_custom_call" | custom-call | tf_op jit(solution)/shard_map/pallas_call | solution.py:69
  130.4 0.0 all-to-all-done.2.refs_0_
  130.4 0.0 copy-start
  130.4 1.2 copy-done
  131.7 3.0 %shard_map.38 = bf16[8,128,128]{2,1,0:T(8,128)(2,1)S(1)} custom-call(bf16[4,8,128,128]{3,2,1,0:T(8,128)(2,1)S(1)} %bitcast.34, bf16[8,2,2,128,256]{4,3,2,1,0:T(8,128)(2,1)S(1)} %all-to-all-done.2.refs_0_), custom_call_target="tpu_custom_call" | custom-call | tf_op jit(solution)/shard_map/pallas_call | solution.py:110
  134.7 3.0 %shard_map.39 = bf16[8,128,128]{2,1,0:T(8,128)(2,1)S(1)} custom-call(bf16[4,8,128,128]{3,2,1,0:T(8,128)(2,1)S(1)} %bitcast.35, bf16[8,2,2,128,256]{4,3,2,1,0:T(8,128)(2,1)S(1)} %all-to-all-done.2.refs_0_), custom_call_target="tpu_custom_call" | custom-call | tf_op jit(solution)/shard_map/pallas_call | solution.py:110
  137.7 0.0 copy-start.1
  137.7 0.1 pad_maximum_fusion.2
  137.8 0.8 copy.27
  138.7 4.9 %all-to-all-start.3 = ((bf16[8,2,128,128]{3,2,1,0:T(8,128)(2,1)}), bf16[8,2,128,128]{3,2,1,0:T(8,128)(2,1)S(1)}, u32[]{:S(2)}, u32[]{:S(2)}) async-start(bf16[8,2,128,128]{3,2,1,0:T(8,128)(2,1)} %copy.27), calls=%async_computation.3 | async-start | bytes 1048576 | tf_op jit(solution)/shard_map/all_to_all | solution.py:31
  143.5 0.0 collective-permute-done.2.refs_1_
  143.5 0.0 copy-done.1
  143.6 4.1 %shard_map.41 = bf16[8,128,128]{2,1,0:T(8,128)(2,1)S(1)} custom-call(bf16[4,8,128,128]{3,2,1,0:T(8,128)(2,1)S(1)} %bitcast.36, bf16[8,2,128,256]{3,2,1,0:T(8,128)(2,1)S(1)} %all-to-all-done.1.refs_0_, bf16[8,128,256]{2,1,0:T(8,128)(2,1)} %collective-permute-done.2.refs_1_), custom_call_target="tpu_custom_call" | custom-call | tf_op jit(solution)/shard_map/pallas_call | solution.py:110
  147.6 0.0 collective-permute-done.1.refs_1_
  147.7 4.1 %shard_map.40 = bf16[8,128,128]{2,1,0:T(8,128)(2,1)S(1)} custom-call(bf16[4,8,128,128]{3,2,1,0:T(8,128)(2,1)S(1)} %bitcast.37, bf16[8,2,128,256]{3,2,1,0:T(8,128)(2,1)S(1)} %all-to-all-done.1.refs_0_, bf16[8,128,256]{2,1,0:T(8,128)(2,1)} %collective-permute-done.1.refs_1_), custom_call_target="tpu_custom_call" | custom-call | tf_op jit(solution)/shard_map/pallas_call | solution.py:110
  151.7 1.3 all-to-all-done.3
  153.0 0.1 pad_maximum_fusion.3
  153.1 12.8 %all_to_all.25 = bf16[8,2,128,128]{3,2,1,0:T(8,128)(2,1)S(1)} all-to-all(bf16[8,2,128,128]{3,2,1,0:T(8,128)(2,1)S(1)} %copy.30), channel_id=1, replica_groups={{0,32,64,96,128,160,192,224},{256,288,320,352,384,416,448,480},{1,33,65..., dimensions={0} | all-to-all | bytes 1048576 | tf_op jit(solution)/shard_map/all_to_all | solution.py:31
  166.0 0.1 pad_maximum_fusion.1
  166.1 1.6 copy.31
  (2 shorter events, 0.1 us)
Async XLA Ops:
  6.5 66.4 %all-gather.6.cloned.1.call-start = ((), (), s32[]{:S(2)}) async-start(), calls=%async_computation.6 | async-start | bytes 7077888 | tf_op jit(solution)/shard_map/all_gather | solution.py:128
  7.3 2.8 %copy-start.3 = (bf16[96,2,128]{2,1,0:T(2,128)(2,1)S(1)}, bf16[96,2,128]{2,1,0:T(2,128)(2,1)}, u32[]{:S(2)}) copy-start(bf16[96,2,128]{2,1,0:T(2,128)(2,1)} %param.4) | copy-start | bytes 147460
  10.8 19.3 %all-to-all-start = ((bf16[8,96,256]{2,1,0:T(8,128)(2,1)}), bf16[8,96,256]{2,1,0:T(8,128)(2,1)S(1)}, u32[]{:S(2)}, u32[]{:S(2)}) async-start(bf16[8,96,256]{2,1,0:T(8,128)(2,1)} %broadcast_in_dim.8), calls=%async_computation | async-start | bytes 786432 | tf_op jit(solution)/shard_map/all_to_all | solution.py:40
  18.5 104.5 %all-gather.4.cloned.1.call-start = ((), (), s32[]{:S(2)}) async-start(), calls=%async_computation.5 | async-start | bytes 3538944 | tf_op jit(solution)/shard_map/all_gather | solution.py:45
  19.7 46.7 %copy-start.2 = (bf16[8,2,128,256]{3,2,1,0:T(8,128)(2,1)}, bf16[8,2,128,256]{3,2,1,0:T(8,128)(2,1)S(1)}, u32[]{:S(2)}) copy-start(bf16[8,2,128,256]{3,2,1,0:T(8,128)(2,1)S(1)} %get-tuple-element.18) | copy-start | bytes 3145732
  31.6 34.8 %collective-permute-start = (bf16[8,2,128,256]{3,2,1,0:T(8,128)(2,1)S(1)}, bf16[8,2,128,256]{3,2,1,0:T(8,128)(2,1)}, u32[]{:S(2)}, u32[]{:S(2)}) collective-permute-start(bf16[8,2,128,256]{3,2,1,0:T(8,128)(2,1)S(1)} %get-tuple-element.18), channel_id=1, source_target_pairs={{0,256},{32,288},{64,320},{96,352},{128,384},{160,416},{192,448},{... | collective-permute-start | bytes 3145736 | tf_op jit(solution)/shard_map/ppermute | solution.py:26
  34.4 34.7 %all-to-all-start.1 = ((bf16[8,2,128,256]{3,2,1,0:T(8,128)(2,1)}), bf16[8,2,128,256]{3,2,1,0:T(8,128)(2,1)S(1)}, u32[]{:S(2)}, u32[]{:S(2)}) async-start(bf16[8,2,128,256]{3,2,1,0:T(8,128)(2,1)} %get-tuple-element.19), calls=%async_computation.1 | async-start | bytes 2097152 | tf_op jit(solution)/shard_map/all_to_all | solution.py:31
  74.3 56.1 %all-to-all-start.2 = ((bf16[8,2,2,128,256]{4,3,2,1,0:T(8,128)(2,1)}), bf16[8,2,2,128,256]{4,3,2,1,0:T(8,128)(2,1)S(1)}, u32[]{:S(2)}, u32[]{:S(2)}) async-start(bf16[8,2,2,128,256]{4,3,2,1,0:T(8,128)(2,1)} %copy.26), calls=%async_computation.2 | async-start | bytes 4194304 | tf_op jit(solution)/shard_map/all_to_all | solution.py:31
  96.9 46.6 %collective-permute-start.2 = (bf16[8,128,256]{2,1,0:T(8,128)(2,1)}, bf16[8,128,256]{2,1,0:T(8,128)(2,1)}, u32[]{:S(2)}, u32[]{:S(2)}) collective-permute-start(bf16[8,128,256]{2,1,0:T(8,128)(2,1)} %get-tuple-element.29), channel_id=1, source_target_pairs={{0,256},{32,288},{64,320},{96,352},{128,384},{160,416},{192,448},{... | collective-permute-start | bytes 1572872 | tf_op jit(solution)/shard_map/ppermute | solution.py:26
  98.9 48.7 %collective-permute-start.1 = (bf16[8,128,256]{2,1,0:T(8,128)(2,1)}, bf16[8,128,256]{2,1,0:T(8,128)(2,1)}, u32[]{:S(2)}, u32[]{:S(2)}) collective-permute-start(bf16[8,128,256]{2,1,0:T(8,128)(2,1)} %get-tuple-element.30), channel_id=1, source_target_pairs={{0,256},{32,288},{64,320},{96,352},{128,384},{160,416},{192,448},{... | collective-permute-start | bytes 1572872 | tf_op jit(solution)/shard_map/ppermute | solution.py:26
  130.4 1.2 copy-start
  137.7 5.8 %copy-start.1 = (bf16[4,1024,128]{2,1,0:T(8,128)(2,1)S(1)}, bf16[4,1024,128]{2,1,0:T(8,128)(2,1)}, u32[]{:S(2)}) copy-start(bf16[4,1024,128]{2,1,0:T(8,128)(2,1)} %shard_map.37) | copy-start | bytes 3145732
  138.7 14.4 %all-to-all-start.3 = ((bf16[8,2,128,128]{3,2,1,0:T(8,128)(2,1)}), bf16[8,2,128,128]{3,2,1,0:T(8,128)(2,1)S(1)}, u32[]{:S(2)}, u32[]{:S(2)}) async-start(bf16[8,2,128,128]{3,2,1,0:T(8,128)(2,1)} %copy.27), calls=%async_computation.3 | async-start | bytes 1048576 | tf_op jit(solution)/shard_map/all_to_all | solution.py:31
Sparse Core Ops, SparseCore 0:
  9.5 63.3 all-gather.5
  75.0 47.9 all-gather.3

commit v5 on v4

--- a/solution.py
+++ b/solution.py
@@ -131,10 +131,13 @@
     block = spread_weight(copies)
 
     spread = jnp.transpose(local_kv.reshape(token_count, HALVES, GROUP, pair, 2 * width), (1, 2, 3, 0, 4))
+    cut = token_count // 4
+    ahead = send(spread[0, :, :, :cut], 1, 0, 0)
     block, lead, rest = together((block, spread[0], spread[1]))
-    lead_far = send(lead, 1, 0, 0)
+    lead_far = send(lead[:, :, cut:], 1, 0, 0)
+    ahead, rest = together((ahead, rest))
     near = within_half(rest)
-    early = jnp.stack([lead, lead_far], axis=1)
+    early = jnp.concatenate([lead, ahead, lead_far], axis=2)
     gathered, early, near = together((gathered, early, near))
     far = [send(near[:, slot], 1, 0, 0) for slot in range(pair)]
     early = within_half(early)
@@ -142,7 +145,7 @@
     block = jnp.transpose(block.reshape(HALVES, RUNS, rows, pair * width), (1, 2, 0, 3))
     weight = gather_ring(block.reshape(RUNS, rows, slots * width))
     queries = project(gathered, weight, slots).reshape(slots, GROUP, token_count, width)
-    outs = [attend(queries, slot, (early, 2)) for slot in range(pair)]
+    outs = [attend(queries, slot, (early, 1)) for slot in range(pair)]
     outs += [attend(queries, pair + slot, (near, 1), (far[slot], None)) for slot in range(pair)]
     first = within_half(jnp.stack(outs[:pair], axis=1))
     first, last = together((first, outs[pair:]))

time: 175 us -> 175 us (level)
  waiting for transfers between devices: 58.1 us -> 43.5 us
  starting transfers between devices: 54.1 us -> 66.1 us
    all_gather x1, waiting for transfers between devices: 16.9 us -> 6.03 us  [gather_ring(): return lax.all_gather(block, 'blk', axis=0, axis_index_groups=rings)]
    ppermute x3 -> x4, starting transfers between devices: 12 us -> 18.4 us  [send(): return lax.ppermute(array, 'uly', pairs)]
    all_to_all x3, waiting for transfers between devices: 2.21 us -> 8.25 us  [within_half(): lax.all_to_all(array, 'uly', 0, 0, tiled=True, axis_index_groups=groups)]
    ppermute x3 -> x4, waiting for transfers between devices: 24.1 us -> 18 us  [send(): return lax.ppermute(array, 'uly', pairs)]
    all_to_all x3, starting transfers between devices: 34.4 us -> 40.1 us  [within_half(): lax.all_to_all(array, 'uly', 0, 0, tiled=True, axis_index_groups=groups)]
    all_gather x1, waiting for transfers between devices: 3.81 us -> 0.01 us  [body(): lax.all_gather(local_tokens, 'uly', axis=0, tiled=True, axis_index_groups...]
    unnamed x10 -> x8, local copies, waits for them, and re-layouts: 4.03 us -> 4.02 us
  transfers between devices with their start and end apart: 9 -> 10, of which waited for: 6 -> 8; matrix products, arithmetic and copies ran while one was open for 6% -> 7% of each run, Pallas kernels for 12% -> 12%
where the time goes in v5:
time: 175 us
  starting transfers between devices  66.1 us (38%)
  waiting for transfers between devices  43.5 us (25%)
  Pallas kernels  21.7 us (12%)
  blocking collectives  14.3 us (8%)
  local copies, waits for them, and re-layouts  13.8 us (8%)
  between operations  13.5 us (8%)
    all_to_all x3, starting transfers between devices, within_half(): lax.all_to_all(array, 'uly', 0, 0, tiled=True, axis_index_groups=groups)  40.1 us
    ppermute x4, starting transfers between devices, send(): return lax.ppermute(array, 'uly', pairs)  18.4 us
    ppermute x4, waiting for transfers between devices, send(): return lax.ppermute(array, 'uly', pairs)  18 us
    all_to_all x1, blocking collectives, within_half(): lax.all_to_all(array, 'uly', 0, 0, tiled=True, axis_index_groups=groups)  14.3 us
    pallas_call x4, Pallas kernels, attend(): pl.pallas_call(attend_kernel, out_shape=jax.ShapeDtypeStruct((members, ro...  14.2 us
    all_to_all x1, waiting for transfers between devices, spread_weight(): lax.all_to_all(copies, ('uly', 'blk'), 0, 0, tiled=True, axis_index_group...  10.4 us
    all_to_all x3, waiting for transfers between devices, within_half(): lax.all_to_all(array, 'uly', 0, 0, tiled=True, axis_index_groups=groups)  8.25 us
    all_to_all x1, starting transfers between devices, spread_weight(): lax.all_to_all(copies, ('uly', 'blk'), 0, 0, tiled=True, axis_index_group...  7.65 us
  transfers between devices with their start and end apart: 10, of which 8 were waited for; matrix products, arithmetic and copies ran while one was open for 7% of the time, Pallas kernels for 12%

profile of v5, /device:TPU:1, one launch (start us, length us, event | category | flops | bytes accessed | tf_op | source)
XLA Modules:
  0.0 174.5 jit_solution(779137139721291268)
XLA Ops:
  6.5 0.0 all-gather.6.cloned.1.call-start
  6.5 0.7 all-gather.6.cloned.1.call-update
  7.3 0.0 copy-start.2
  7.3 2.8 %copy.35 = bf16[1,128,32,256]{3,1,2,0:T(8,128)(2,1)S(1)} copy(bf16[1,128,32,256]{3,2,1,0:T(8,128)(2,1)} %param.5) | data formatting | bytes 4194304 | tf_op args[2]
  10.0 0.0 copy-done.2
  10.1 0.8 broadcast_in_dim.8
  10.8 7.7 %all-to-all-start = ((bf16[8,96,256]{2,1,0:T(8,128)(2,1)}), bf16[8,96,256]{2,1,0:T(8,128)(2,1)S(1)}, u32[]{:S(2)}, u32[]{:S(2)}) async-start(bf16[8,96,256]{2,1,0:T(8,128)(2,1)} %broadcast_in_dim.8), calls=%async_computation | async-start | bytes 786432 | tf_op jit(solution)/shard_map/all_to_all | solution.py:40
  18.5 0.0 all-gather.4.cloned.1.call-start
  18.5 1.2 slice_bitcast_fusion
  19.7 10.4 %all-to-all-done = bf16[8,96,256]{2,1,0:T(8,128)(2,1)S(1)} async-done(((bf16[8,96,256]{2,1,0:T(8,128)(2,1)}), bf16[8,96,256]{2,1,0:T(8,128)(2,1)S(1)}, u32[]{:S(2)}, u32[]{:S(2)}) %all-to-all-start) | async-done | bytes 393248 | tf_op jit(solution)/shard_map/all_to_all | solution.py:40
  30.1 1.2 copy.24
  31.3 2.1 %all_gather_reshape.3 = bf16[1,4,96,512]{3,2,1,0:T(8,128)(2,1)} reshape(bf16[4,96,2,256]{3,2,1,0:T(2,128)(2,1)} %copy.24) | data formatting | bytes 786432 | tf_op jit(solution)/shard_map/all_gather;reshape | solution.py:45
  33.4 0.0 all-gather.4.cloned.1.call-update
  33.5 2.7 %collective-permute-start = (bf16[8,2,32,256]{3,2,1,0:T(8,128)(2,1)S(1)}, bf16[8,2,32,256]{3,2,1,0:T(8,128)(2,1)S(1)}, u32[]{:S(2)}, u32[]{:S(2)}) collective-permute-start(bf16[8,2,32,256]{3,2,1,0:T(8,128)(2,1)S(1)} %slice_bitcast_fusion.4), channel_id=1, source_target_pairs={{0,256},{32,288},{64,320},{96,352},{128,384},{160,416},{192,448},{... | collective-permute-start | bytes 786440 | tf_op jit(solution)/shard_map/ppermute | solution.py:26
  36.1 1.0 slice.21
  37.1 6.5 %collective-permute-start.1 = (bf16[8,2,96,256]{3,2,1,0:T(8,128)(2,1)}, bf16[8,2,96,256]{3,2,1,0:T(8,128)(2,1)S(1)}, u32[]{:S(2)}, u32[]{:S(2)}) collective-permute-start(bf16[8,2,96,256]{3,2,1,0:T(8,128)(2,1)} %slice.21), channel_id=1, source_target_pairs={{0,256},{32,288},{64,320},{96,352},{128,384},{160,416},{192,448},{... | collective-permute-start | bytes 2359304 | tf_op jit(solution)/shard_map/ppermute | solution.py:26
  43.6 1.0 collective-permute-done
  44.6 22.1 %all-to-all-start.1 = ((bf16[8,2,128,256]{3,2,1,0:T(8,128)(2,1)}), bf16[8,2,128,256]{3,2,1,0:T(8,128)(2,1)S(1)}, u32[]{:S(2)}, u32[]{:S(2)}) async-start(bf16[8,2,128,256]{3,2,1,0:T(8,128)(2,1)} %get-tuple-element.23), calls=%async_computation.1 | async-start | bytes 2097152 | tf_op jit(solution)/shard_map/all_to_all | solution.py:31
  66.7 8.1 %collective-permute-done.1 = bf16[8,2,96,256]{3,2,1,0:T(8,128)(2,1)S(1)} collective-permute-done((bf16[8,2,96,256]{3,2,1,0:T(8,128)(2,1)}, bf16[8,2,96,256]{3,2,1,0:T(8,128)(2,1)S(1)}, u32[]{:S(2)}, u32[]{:S(2)}) %collective-permute-start.1) | collective-permute-done | bytes 786464 | tf_op jit(solution)/shard_map/ppermute | solution.py:26
  74.8 1.4 pad_maximum_fusion
  76.2 5.6 %all-to-all-done.1.refs_0_ = bf16[8,2,128,256]{3,2,1,0:T(8,128)(2,1)S(1)} async-done(((bf16[8,2,128,256]{3,2,1,0:T(8,128)(2,1)}), bf16[8,2,128,256]{3,2,1,0:T(8,128)(2,1)S(1)}, u32[]{:S(2)}, u32[]{:S(2)}) %all-to-all-start.1) | async-done | bytes 1048608 | tf_op jit(solution)/shard_map/all_to_all | solution.py:31
  81.8 0.0 all-gather.6.cloned.1.call-done
  81.8 13.9 %all-to-all-start.2 = ((bf16[8,2,256,256]{3,2,1,0:T(8,128)(2,1)}), bf16[8,2,256,256]{3,2,1,0:T(8,128)(2,1)S(1)}, u32[]{:S(2)}, u32[]{:S(2)}) async-start(bf16[8,2,256,256]{3,2,1,0:T(8,128)(2,1)} %pad_maximum_fusion), calls=%async_computation.2 | async-start | bytes 4194304 | tf_op jit(solution)/shard_map/all_to_all | solution.py:31
  95.6 1.1 slice_bitcast_fusion.2
  96.7 2.1 %collective-permute-start.3 = (bf16[8,128,256]{2,1,0:T(8,128)(2,1)}, bf16[8,128,256]{2,1,0:T(8,128)(2,1)}, u32[]{:S(2)}, u32[]{:S(2)}) collective-permute-start(bf16[8,128,256]{2,1,0:T(8,128)(2,1)} %get-tuple-element.33), channel_id=1, source_target_pairs={{0,256},{32,288},{64,320},{96,352},{128,384},{160,416},{192,448},{... | collective-permute-start | bytes 1572872 | tf_op jit(solution)/shard_map/ppermute | solution.py:26
  98.8 7.1 %collective-permute-start.2 = (bf16[8,128,256]{2,1,0:T(8,128)(2,1)}, bf16[8,128,256]{2,1,0:T(8,128)(2,1)}, u32[]{:S(2)}, u32[]{:S(2)}) collective-permute-start(bf16[8,128,256]{2,1,0:T(8,128)(2,1)} %get-tuple-element.34), channel_id=1, source_target_pairs={{0,256},{32,288},{64,320},{96,352},{128,384},{160,416},{192,448},{... | collective-permute-start | bytes 1572872 | tf_op jit(solution)/shard_map/ppermute | solution.py:26
  105.9 6.0 %all-gather.4.cloned.1.call-done.weight_ref = bf16[8,4,96,512]{3,2,1,0:T(8,128)(2,1)} async-done(((bf16[1,4,96,512]{3,2,1,0:T(8,128)(2,1)}), bf16[8,4,96,512]{3,2,1,0:T(8,128)(2,1)}) %all-gather.4.cloned.1.call-update) | async-done | bytes 3145744 | tf_op jit(solution)/shard_map/all_gather | solution.py:45
  111.9 7.4 %shard_map.37 = bf16[4,1024,128]{2,1,0:T(8,128)(2,1)} custom-call(bf16[1024,3072]{1,0:T(8,128)(2,1)} %bitcast.44, bf16[8,4,96,512]{3,2,1,0:T(8,128)(2,1)} %all-gather.4.cloned.1.call-done.weight_ref), custom_call_target="tpu_custom_call" | custom-call | tf_op jit(solution)/shard_map/pallas_call | solution.py:69
  119.4 2.7 %all-to-all-done.2.refs_0_ = bf16[8,2,256,256]{3,2,1,0:T(8,128)(2,1)S(1)} async-done(((bf16[8,2,256,256]{3,2,1,0:T(8,128)(2,1)}), bf16[8,2,256,256]{3,2,1,0:T(8,128)(2,1)S(1)}, u32[]{:S(2)}, u32[]{:S(2)}) %all-to-all-start.2) | async-done | bytes 2097184 | tf_op jit(solution)/shard_map/all_to_all | solution.py:31
  122.1 0.0 copy-start
  122.1 1.2 copy-done
  123.3 3.0 %shard_map.38 = bf16[8,128,128]{2,1,0:T(8,128)(2,1)S(1)} custom-call(bf16[4,8,128,128]{3,2,1,0:T(8,128)(2,1)S(1)} %bitcast.34, bf16[8,2,256,256]{3,2,1,0:T(8,128)(2,1)S(1)} %all-to-all-done.2.refs_0_), custom_call_target="tpu_custom_call" | custom-call | tf_op jit(solution)/shard_map/pallas_call | solution.py:110
  126.3 3.0 %shard_map.39 = bf16[8,128,128]{2,1,0:T(8,128)(2,1)S(1)} custom-call(bf16[4,8,128,128]{3,2,1,0:T(8,128)(2,1)S(1)} %bitcast.35, bf16[8,2,256,256]{3,2,1,0:T(8,128)(2,1)S(1)} %all-to-all-done.2.refs_0_), custom_call_target="tpu_custom_call" | custom-call | tf_op jit(solution)/shard_map/pallas_call | solution.py:110
  129.4 0.0 copy-start.1
  129.4 0.1 pad_maximum_fusion.2
  129.5 0.8 copy.25
  130.3 4.2 %all-to-all-start.3 = ((bf16[8,2,128,128]{3,2,1,0:T(8,128)(2,1)}), bf16[8,2,128,128]{3,2,1,0:T(8,128)(2,1)S(1)}, u32[]{:S(2)}, u32[]{:S(2)}) async-start(bf16[8,2,128,128]{3,2,1,0:T(8,128)(2,1)} %copy.25), calls=%async_computation.3 | async-start | bytes 1048576 | tf_op jit(solution)/shard_map/all_to_all | solution.py:31
  134.5 1.7 %collective-permute-done.3.refs_1_ = bf16[8,128,256]{2,1,0:T(8,128)(2,1)} collective-permute-done((bf16[8,128,256]{2,1,0:T(8,128)(2,1)}, bf16[8,128,256]{2,1,0:T(8,128)(2,1)}, u32[]{:S(2)}, u32[]{:S(2)}) %collective-permute-start.3) | collective-permute-done | bytes 524320 | tf_op jit(solution)/shard_map/ppermute | solution.py:26
  136.2 0.0 copy-done.1
  136.2 4.1 %shard_map.41 = bf16[8,128,128]{2,1,0:T(8,128)(2,1)S(1)} custom-call(bf16[4,8,128,128]{3,2,1,0:T(8,128)(2,1)S(1)} %bitcast.36, bf16[8,2,128,256]{3,2,1,0:T(8,128)(2,1)S(1)} %all-to-all-done.1.refs_0_, bf16[8,128,256]{2,1,0:T(8,128)(2,1)} %collective-permute-done.3.refs_1_), custom_call_target="tpu_custom_call" | custom-call | tf_op jit(solution)/shard_map/pallas_call | solution.py:110
  140.3 7.1 %collective-permute-done.2.refs_1_ = bf16[8,128,256]{2,1,0:T(8,128)(2,1)} collective-permute-done((bf16[8,128,256]{2,1,0:T(8,128)(2,1)}, bf16[8,128,256]{2,1,0:T(8,128)(2,1)}, u32[]{:S(2)}, u32[]{:S(2)}) %collective-permute-start.2) | collective-permute-done | bytes 524320 | tf_op jit(solution)/shard_map/ppermute | solution.py:26
  147.4 4.1 %shard_map.40 = bf16[8,128,128]{2,1,0:T(8,128)(2,1)S(1)} custom-call(bf16[4,8,128,128]{3,2,1,0:T(8,128)(2,1)S(1)} %bitcast.37, bf16[8,2,128,256]{3,2,1,0:T(8,128)(2,1)S(1)} %all-to-all-done.1.refs_0_, bf16[8,128,256]{2,1,0:T(8,128)(2,1)} %collective-permute-done.2.refs_1_), custom_call_target="tpu_custom_call" | custom-call | tf_op jit(solution)/shard_map/pallas_call | solution.py:110
  151.5 0.0 all-to-all-done.3
  151.5 0.1 pad_maximum_fusion.3
  151.7 14.3 %all_to_all.25 = bf16[8,2,128,128]{3,2,1,0:T(8,128)(2,1)S(1)} all-to-all(bf16[8,2,128,128]{3,2,1,0:T(8,128)(2,1)S(1)} %copy.28), channel_id=1, replica_groups={{0,32,64,96,128,160,192,224},{256,288,320,352,384,416,448,480},{1,33,65..., dimensions={0} | all-to-all | bytes 1048576 | tf_op jit(solution)/shard_map/all_to_all | solution.py:31
  165.9 0.1 pad_maximum_fusion.1
  166.0 1.6 copy.29
  (3 shorter events, 0.1 us)
Async XLA Ops:
  6.5 75.3 %all-gather.6.cloned.1.call-start = ((), (), s32[]{:S(2)}) async-start(), calls=%async_computation.6 | async-start | bytes 7077888 | tf_op jit(solution)/shard_map/all_gather | solution.py:128
  7.3 2.8 %copy-start.2 = (bf16[96,2,128]{2,1,0:T(2,128)(2,1)S(1)}, bf16[96,2,128]{2,1,0:T(2,128)(2,1)}, u32[]{:S(2)}) copy-start(bf16[96,2,128]{2,1,0:T(2,128)(2,1)} %param.4) | copy-start | bytes 147460
  10.8 19.3 %all-to-all-start = ((bf16[8,96,256]{2,1,0:T(8,128)(2,1)}), bf16[8,96,256]{2,1,0:T(8,128)(2,1)S(1)}, u32[]{:S(2)}, u32[]{:S(2)}) async-start(bf16[8,96,256]{2,1,0:T(8,128)(2,1)} %broadcast_in_dim.8), calls=%async_computation | async-start | bytes 786432 | tf_op jit(solution)/shard_map/all_to_all | solution.py:40
  18.5 93.4 %all-gather.4.cloned.1.call-start = ((), (), s32[]{:S(2)}) async-start(), calls=%async_computation.5 | async-start | bytes 3538944 | tf_op jit(solution)/shard_map/all_gather | solution.py:45
  33.5 11.2 %collective-permute-start = (bf16[8,2,32,256]{3,2,1,0:T(8,128)(2,1)S(1)}, bf16[8,2,32,256]{3,2,1,0:T(8,128)(2,1)S(1)}, u32[]{:S(2)}, u32[]{:S(2)}) collective-permute-start(bf16[8,2,32,256]{3,2,1,0:T(8,128)(2,1)S(1)} %slice_bitcast_fusion.4), channel_id=1, source_target_pairs={{0,256},{32,288},{64,320},{96,352},{128,384},{160,416},{192,448},{... | collective-permute-start | bytes 786440 | tf_op jit(solution)/shard_map/ppermute | solution.py:26
  37.1 37.7 %collective-permute-start.1 = (bf16[8,2,96,256]{3,2,1,0:T(8,128)(2,1)}, bf16[8,2,96,256]{3,2,1,0:T(8,128)(2,1)S(1)}, u32[]{:S(2)}, u32[]{:S(2)}) collective-permute-start(bf16[8,2,96,256]{3,2,1,0:T(8,128)(2,1)} %slice.21), channel_id=1, source_target_pairs={{0,256},{32,288},{64,320},{96,352},{128,384},{160,416},{192,448},{... | collective-permute-start | bytes 2359304 | tf_op jit(solution)/shard_map/ppermute | solution.py:26
  44.6 37.2 %all-to-all-start.1 = ((bf16[8,2,128,256]{3,2,1,0:T(8,128)(2,1)}), bf16[8,2,128,256]{3,2,1,0:T(8,128)(2,1)S(1)}, u32[]{:S(2)}, u32[]{:S(2)}) async-start(bf16[8,2,128,256]{3,2,1,0:T(8,128)(2,1)} %get-tuple-element.23), calls=%async_computation.1 | async-start | bytes 2097152 | tf_op jit(solution)/shard_map/all_to_all | solution.py:31
  81.8 40.3 %all-to-all-start.2 = ((bf16[8,2,256,256]{3,2,1,0:T(8,128)(2,1)}), bf16[8,2,256,256]{3,2,1,0:T(8,128)(2,1)S(1)}, u32[]{:S(2)}, u32[]{:S(2)}) async-start(bf16[8,2,256,256]{3,2,1,0:T(8,128)(2,1)} %pad_maximum_fusion), calls=%async_computation.2 | async-start | bytes 4194304 | tf_op jit(solution)/shard_map/all_to_all | solution.py:31
  96.7 39.5 %collective-permute-start.3 = (bf16[8,128,256]{2,1,0:T(8,128)(2,1)}, bf16[8,128,256]{2,1,0:T(8,128)(2,1)}, u32[]{:S(2)}, u32[]{:S(2)}) collective-permute-start(bf16[8,128,256]{2,1,0:T(8,128)(2,1)} %get-tuple-element.33), channel_id=1, source_target_pairs={{0,256},{32,288},{64,320},{96,352},{128,384},{160,416},{192,448},{... | collective-permute-start | bytes 1572872 | tf_op jit(solution)/shard_map/ppermute | solution.py:26
  98.8 48.6 %collective-permute-start.2 = (bf16[8,128,256]{2,1,0:T(8,128)(2,1)}, bf16[8,128,256]{2,1,0:T(8,128)(2,1)}, u32[]{:S(2)}, u32[]{:S(2)}) collective-permute-start(bf16[8,128,256]{2,1,0:T(8,128)(2,1)} %get-tuple-element.34), channel_id=1, source_target_pairs={{0,256},{32,288},{64,320},{96,352},{128,384},{160,416},{192,448},{... | collective-permute-start | bytes 1572872 | tf_op jit(solution)/shard_map/ppermute | solution.py:26
  122.1 1.2 copy-start
  129.4 6.8 %copy-start.1 = (bf16[4,1024,128]{2,1,0:T(8,128)(2,1)S(1)}, bf16[4,1024,128]{2,1,0:T(8,128)(2,1)}, u32[]{:S(2)}) copy-start(bf16[4,1024,128]{2,1,0:T(8,128)(2,1)} %shard_map.37) | copy-start | bytes 3145732
  130.3 21.2 %all-to-all-start.3 = ((bf16[8,2,128,128]{3,2,1,0:T(8,128)(2,1)}), bf16[8,2,128,128]{3,2,1,0:T(8,128)(2,1)S(1)}, u32[]{:S(2)}, u32[]{:S(2)}) async-start(bf16[8,2,128,128]{3,2,1,0:T(8,128)(2,1)} %copy.25), calls=%async_computation.3 | async-start | bytes 1048576 | tf_op jit(solution)/shard_map/all_to_all | solution.py:31
Sparse Core Ops, SparseCore 0:
  9.5 52.1 all-gather.5
  63.7 48.1 all-gather.3
